TPU v7x, 512 devices: a whole 4x4x16 slice. The times are simulated.
512 devices in a mesh: line: 128 (over z, x, core), tm: 4 (over y).
Axes of the slice: x: 4, y: 4, z: 16, core: 2. Of those that a mesh axis runs over, the one named last changes fastest.
Arguments:
- traces: float32 [128, 512, 4, 512], P('line', None, None, 'tm'), may hold values from -40 to 40
- rates: int32 [128, 4, 8, 32], P('line', 'tm'), may hold values from 16 to 188
- byte_target: int32 [1], replicated, may hold values from 160 to 319
Outputs:
- coefficients: float32 [32, 2048, 4, 512], P(None, 'line', None, 'tm')
All inputs are finite; a program needn't handle non-finite values.
Results may differ from a plain program's by a relative error of at most 0.0003.
Values sent between devices are 32-bit elements; how exact they have to be, the bound alone decides.
A program may use at most 64 MiB of HBM per device.

v0:
```python
import jax
import jax.numpy as jnp
from jax import lax
from jax.sharding import PartitionSpec as P

PLANES = 8
BISECT = 12


slope_floor = -12.0
slope_span = 32.0
rate_scale = 65536.0


def shifted(value, axis, steps):
    count = lax.axis_size(axis)
    initial, last = (max(0, -steps), min(count, count - steps))
    return lax.ppermute(value, axis, [(source, source + steps) for source in range(initial, last)])


def detail(even_part, odd_part, ahead_even):
    return odd_part - 0.5 * (even_part + ahead_even)


def smooth(even_part, behind, details):
    return even_part + 0.25 * (behind + details)


def time_ahead(values):
    return shifted(values, "tm", -1)


def time_behind(values):
    return shifted(values, "tm", 1)


def line_ahead(values):
    return shifted(values, "line", -1)


def line_behind(values):
    return shifted(values, "line", 1)


def time_first(signal):
    phase_zero, phase_one, phase_two, phase_three = (
        signal[:, :, 0],
        signal[:, :, 1],
        signal[:, :, 2],
        signal[:, :, 3],
    )
    ahead_even = jnp.concatenate([phase_zero[:, :, 1:], time_ahead(phase_zero[:, :, :1])], axis=2)
    detail_one = detail(phase_zero, phase_one, phase_two)
    detail_three = detail(phase_two, phase_three, ahead_even)
    behind = jnp.concatenate(
        [time_behind(detail_three[:, :, -1:]), detail_three[:, :, :-1]], axis=2
    )
    smooth_zero = smooth(phase_zero, behind, detail_one)
    smooth_two = smooth(phase_two, detail_one, detail_three)
    return jnp.stack([smooth_zero, detail_one, smooth_two, detail_three], axis=2)


def time_pair(even_part, odd_part):
    ahead_even = jnp.concatenate([even_part[:, :, 1:], time_ahead(even_part[:, :, :1])], axis=2)
    details = detail(even_part, odd_part, ahead_even)
    behind = jnp.concatenate([time_behind(details[:, :, -1:]), details[:, :, :-1]], axis=2)
    return (smooth(even_part, behind, details), details)


def line_rims(even_part, odd_part):
    ahead_even = jnp.concatenate([even_part[:, 1:], line_ahead(even_part[:, :1])], axis=1)
    details = detail(even_part, odd_part, ahead_even)
    behind = jnp.concatenate([line_behind(details[:, -1:]), details[:, :-1]], axis=1)
    return (details, behind)


def receiver_lift(series):
    even_part = series[:, 0::2]
    odd_part = series[:, 1::2]
    details, behind = line_rims(even_part, odd_part)
    lowpass = smooth(even_part, behind, details)
    return jnp.stack([lowpass, details], axis=2).reshape(series.shape)


def finish(signal):
    lifted = receiver_lift(signal)
    rows_even = lifted[:, 0::2]
    rows_odd = lifted[:, 1::2]
    lowpass, details = time_pair(rows_even[:, :, 0], rows_even[:, :, 2])
    band_two = receiver_lift(jnp.stack([lowpass, details], axis=2))
    even_new = jnp.stack(
        [band_two[:, :, 0], rows_even[:, :, 1], band_two[:, :, 1], rows_even[:, :, 3]], axis=2
    )
    return jnp.stack([even_new, rows_odd], axis=2).reshape(lifted.shape)


def slope_at(grid_index):
    return jnp.exp2(slope_floor + grid_index.astype(jnp.float32) * (slope_span / 2**BISECT))


def body(traces, rates, byte_target):
    line_count = lax.axis_size("line")
    band_count = lax.axis_size("tm")
    block_width = traces.shape[3]
    group_width = traces.shape[1] // line_count
    rec_dev = 4 * group_width
    shot_count = line_count // 4
    parted = traces.reshape(1, line_count, group_width, 4, block_width)
    item_block = lax.all_to_all(parted, "line", split_axis=1, concat_axis=0, tiled=True)
    flattened = item_block.reshape(item_block.shape[0], item_block.shape[2], 4, block_width)
    regrouped = time_first(flattened).reshape(item_block.shape)
    wavelet = finish(regrouped.reshape(shot_count, rec_dev, 4, block_width))
    square = wavelet * wavelet
    planes_out = []
    for plane_index in range(PLANES):
        bottom_sq = 4.0 ** (3 - plane_index)
        top_sq = 4.0 ** (4 - plane_index)
        planes_out.append(jnp.sum(jnp.clip(square, bottom_sq, top_sq) - bottom_sq, axis=(1, 2, 3)))
    plane_gain = jnp.stack(planes_out)
    rate_table = rates.reshape(rates.shape[2], rates.shape[3])
    rate_float = rate_table.astype(jnp.float32)
    byte_limit = byte_target[0] * (wavelet.shape[0] * line_count * band_count)

    def bisect_turn(turn_index, bounds):
        bottom, ceiling = bounds
        middle = (bottom + ceiling) // 2
        chosen_rates = jnp.where(plane_gain >= slope_at(middle) * rate_float, rate_table, 0)
        local_kept = jnp.sum(chosen_rates, dtype=jnp.int32)
        total_kept = lax.psum(local_kept, ("line", "tm"))
        within = total_kept <= byte_limit
        return (jnp.where(within, bottom, middle), jnp.where(within, middle, ceiling))

    bottom, ceiling = lax.fori_loop(0, BISECT, bisect_turn, (jnp.int32(0), jnp.int32(2**BISECT)))
    slope_now = slope_at(ceiling)
    rate_sums = jnp.sum(rate_table, axis=0).astype(jnp.float32)
    shrink_by = jnp.sqrt(slope_now * rate_sums / rate_scale)[:, None, None, None]
    return wavelet - jnp.clip(wavelet, -shrink_by, shrink_by)


def solution(mesh):
    return jax.shard_map(
        body,
        mesh=mesh,
        in_specs=(P("line", None, None, "tm"), P("line", "tm", None, None), P()),
        out_specs=P(None, "line", None, "tm"),
        check_vma=False,
    )
```

profile of v0, /device:TPU:1, one launch (start us, length us, event | category | flops | bytes accessed | tf_op | source)
XLA Modules:
  0.0 1353.2 jit_solution(3590238452668634063)
XLA Ops:
  1.5 72.0 %all_to_all.4 = f32[1,128,4,4,128]{4,2,3,0,1:T(4,128)S(1)} all-to-all(f32[1,128,4,4,128]{4,2,3,0,1:T(4,128)S(1)} %copy.94), channel_id=1, replica_groups=mesh['line'=128,'tm'=4] {'line'}, dimensions={1} | all-to-all | bytes 2097152 | tf_op jit(solution)/shard_map/all_to_all | solution.py:109
  75.7 5.3 collective-permute-done
  81.3 3.2 collective-permute-start.1
  84.6 3.3 collective-permute-done.1
  89.2 6.4 collective-permute-start.2
  95.9 5.9 collective-permute-done.2
  102.1 1.9 collective-permute-start.3
  107.3 6.5 collective-permute-done.4
  114.0 3.2 collective-permute-start.5
  119.3 3.7 collective-permute-start.6
  123.0 3.4 collective-permute-done.6
  130.8 1220.4 %while.14 = (s32[]{:T(128)}, s32[]{:T(128)}, s32[]{:T(128)}, f32[8,32]{1,0:T(8,128)S(1)}, f32[8,32]{1,0:T(8,128)S(1)}, /*index=5*/s32[8,32]{1,0:T(8,128)S(1)}, s...) while((s32[]{:T(128)}, s32[]{:T(128)}, s32[]{:T(128)}, ...), condition=%wide.region_11.12_spmd, body=%wide.region_8.11_spmd.sunk | while | flops 1049 | bytes 3462 | solution.py:133
  131.5 105.9 %psum.11 = s32[]{:T(128)} all-reduce(s32[]{:T(128)} %select_reduce_fusion.2), channel_id=1, replica_groups=mesh['line'=128,'tm'=4] {'line','tm'}, use_global_device_ids=true, to_apply=%region_10.10 | all-reduce | flops 1 | bytes 8 | tf_op jit(solution)/shard_map/while/body/eval_jaxpr/psum | solution.py:129
  238.7 101.2 %psum.11 = s32[]{:T(128)} all-reduce(s32[]{:T(128)} %select_reduce_fusion.2), channel_id=1, replica_groups=mesh['line'=128,'tm'=4] {'line','tm'}, use_global_device_ids=true, to_apply=%region_10.10 | all-reduce | flops 1 | bytes 8 | tf_op jit(solution)/shard_map/while/body/eval_jaxpr/psum | solution.py:129
  341.2 99.2 %psum.11 = s32[]{:T(128)} all-reduce(s32[]{:T(128)} %select_reduce_fusion.2), channel_id=1, replica_groups=mesh['line'=128,'tm'=4] {'line','tm'}, use_global_device_ids=true, to_apply=%region_10.10 | all-reduce | flops 1 | bytes 8 | tf_op jit(solution)/shard_map/while/body/eval_jaxpr/psum | solution.py:129
  441.7 100.3 %psum.11 = s32[]{:T(128)} all-reduce(s32[]{:T(128)} %select_reduce_fusion.2), channel_id=1, replica_groups=mesh['line'=128,'tm'=4] {'line','tm'}, use_global_device_ids=true, to_apply=%region_10.10 | all-reduce | flops 1 | bytes 8 | tf_op jit(solution)/shard_map/while/body/eval_jaxpr/psum | solution.py:129
  543.3 99.4 %psum.11 = s32[]{:T(128)} all-reduce(s32[]{:T(128)} %select_reduce_fusion.2), channel_id=1, replica_groups=mesh['line'=128,'tm'=4] {'line','tm'}, use_global_device_ids=true, to_apply=%region_10.10 | all-reduce | flops 1 | bytes 8 | tf_op jit(solution)/shard_map/while/body/eval_jaxpr/psum | solution.py:129
  644.0 100.1 %psum.11 = s32[]{:T(128)} all-reduce(s32[]{:T(128)} %select_reduce_fusion.2), channel_id=1, replica_groups=mesh['line'=128,'tm'=4] {'line','tm'}, use_global_device_ids=true, to_apply=%region_10.10 | all-reduce | flops 1 | bytes 8 | tf_op jit(solution)/shard_map/while/body/eval_jaxpr/psum | solution.py:129
  745.4 99.4 %psum.11 = s32[]{:T(128)} all-reduce(s32[]{:T(128)} %select_reduce_fusion.2), channel_id=1, replica_groups=mesh['line'=128,'tm'=4] {'line','tm'}, use_global_device_ids=true, to_apply=%region_10.10 | all-reduce | flops 1 | bytes 8 | tf_op jit(solution)/shard_map/while/body/eval_jaxpr/psum | solution.py:129
  846.0 100.2 %psum.11 = s32[]{:T(128)} all-reduce(s32[]{:T(128)} %select_reduce_fusion.2), channel_id=1, replica_groups=mesh['line'=128,'tm'=4] {'line','tm'}, use_global_device_ids=true, to_apply=%region_10.10 | all-reduce | flops 1 | bytes 8 | tf_op jit(solution)/shard_map/while/body/eval_jaxpr/psum | solution.py:129
  947.5 99.4 %psum.11 = s32[]{:T(128)} all-reduce(s32[]{:T(128)} %select_reduce_fusion.2), channel_id=1, replica_groups=mesh['line'=128,'tm'=4] {'line','tm'}, use_global_device_ids=true, to_apply=%region_10.10 | all-reduce | flops 1 | bytes 8 | tf_op jit(solution)/shard_map/while/body/eval_jaxpr/psum | solution.py:129
  1048.2 100.2 %psum.11 = s32[]{:T(128)} all-reduce(s32[]{:T(128)} %select_reduce_fusion.2), channel_id=1, replica_groups=mesh['line'=128,'tm'=4] {'line','tm'}, use_global_device_ids=true, to_apply=%region_10.10 | all-reduce | flops 1 | bytes 8 | tf_op jit(solution)/shard_map/while/body/eval_jaxpr/psum | solution.py:129
  1149.7 99.4 %psum.11 = s32[]{:T(128)} all-reduce(s32[]{:T(128)} %select_reduce_fusion.2), channel_id=1, replica_groups=mesh['line'=128,'tm'=4] {'line','tm'}, use_global_device_ids=true, to_apply=%region_10.10 | all-reduce | flops 1 | bytes 8 | tf_op jit(solution)/shard_map/while/body/eval_jaxpr/psum | solution.py:129
  1250.4 100.2 %psum.11 = s32[]{:T(128)} all-reduce(s32[]{:T(128)} %select_reduce_fusion.2), channel_id=1, replica_groups=mesh['line'=128,'tm'=4] {'line','tm'}, use_global_device_ids=true, to_apply=%region_10.10 | all-reduce | flops 1 | bytes 8 | tf_op jit(solution)/shard_map/while/body/eval_jaxpr/psum | solution.py:129
  (70 shorter events, 24.5 us)
Async XLA Ops:
  73.9 7.1 collective-permute-start
  81.3 6.5 collective-permute-start.1
  89.2 12.6 collective-permute-start.2
  102.1 3.2 collective-permute-start.3
  105.9 7.9 collective-permute-start.4
  114.0 5.1 collective-permute-start.5
  119.3 7.1 collective-permute-start.6
  126.4 2.0 copy-start
  126.5 3.1 collective-permute-start.7
where the time goes:
time: 1360 us; the launch traced here: 1350 us
  blocking collectives  1280 us (94%)
  waiting for transfers between devices  28.1 us (2%)
  starting transfers between devices  22.8 us (2%)
    psum x12, blocking collectives, bisect_turn(): total_kept = lax.psum(local_kept, ('line', 'tm'))  1200 us
    all_to_all x1, blocking collectives, body(): lax.all_to_all(parted, 'line', split_axis=1, concat_axis=0, tiled=True)  72 us
    ppermute x8, waiting for transfers between devices, shifted(): lax.ppermute(value, axis, [(source, source + steps) for source in range(i...  28.1 us
  transfers between devices with their start and end apart: 8, of which 8 were waited for; matrix products, arithmetic and copies ran while one was open for 0% of the time, Pallas kernels for 0%

commit v1 on v0

--- a/solution.py
+++ b/solution.py
@@ -1,11 +1,13 @@
 import jax
 import jax.numpy as jnp
 from jax import lax
+from jax.experimental import pallas as pl
+from jax.experimental.pallas import tpu as pltpu
 from jax.sharding import PartitionSpec as P
 
 PLANES = 8
 BISECT = 12
-
+MESH = pl.DeviceIdType.MESH
 
 slope_floor = -12.0
 slope_span = 32.0
@@ -98,18 +100,58 @@
     return jnp.exp2(slope_floor + grid_index.astype(jnp.float32) * (slope_span / 2**BISECT))
 
 
+def regroup_kernel(x_ref, o_ref, ssem, rsem, lsem):
+    n = 128
+    me = lax.axis_index("line")
+    bar = pltpu.get_barrier_semaphore()
+
+    @pl.loop(0, n - 1)
+    def _(i):
+        pl.semaphore_signal(
+            bar, inc=1, device_id={"line": lax.rem(me + i + 1, n)}, device_id_type=MESH
+        )
+
+    pl.semaphore_wait(bar, n - 1)
+    mine = o_ref.at[pl.ds(pl.multiple_of(me * 16, 16), 16)]
+
+    @pl.loop(0, n - 1)
+    def _(i):
+        target = lax.rem(me + i + 1, n)
+        pltpu.make_async_remote_copy(
+            src_ref=x_ref.at[pl.ds(pl.multiple_of(target * 16, 16), 16)],
+            dst_ref=mine,
+            send_sem=ssem,
+            recv_sem=rsem,
+            device_id={"line": target},
+            device_id_type=MESH,
+        ).start()
+
+    own = pltpu.make_async_copy(x_ref.at[pl.ds(pl.multiple_of(me * 16, 16), 16)], mine, lsem)
+    own.start()
+    own.wait()
+    most = o_ref.at[pl.ds(0, (n - 1) * 16)]
+    pltpu.make_async_copy(most, most, rsem).wait()
+    pltpu.make_async_copy(most, most, ssem).wait()
+
+
+def regroup(rows):
+    return pl.pallas_call(
+        regroup_kernel,
+        out_shape=jax.ShapeDtypeStruct(rows.shape, rows.dtype),
+        in_specs=[pl.BlockSpec(memory_space=pl.ANY)],
+        out_specs=pl.BlockSpec(memory_space=pl.ANY),
+        scratch_shapes=[pltpu.SemaphoreType.DMA] * 3,
+        compiler_params=pltpu.CompilerParams(collective_id=1, has_side_effects=True),
+        name="regroup",
+    )(rows)
+
+
 def body(traces, rates, byte_target):
     line_count = lax.axis_size("line")
     band_count = lax.axis_size("tm")
-    block_width = traces.shape[3]
-    group_width = traces.shape[1] // line_count
-    rec_dev = 4 * group_width
-    shot_count = line_count // 4
-    parted = traces.reshape(1, line_count, group_width, 4, block_width)
-    item_block = lax.all_to_all(parted, "line", split_axis=1, concat_axis=0, tiled=True)
-    flattened = item_block.reshape(item_block.shape[0], item_block.shape[2], 4, block_width)
-    regrouped = time_first(flattened).reshape(item_block.shape)
-    wavelet = finish(regrouped.reshape(shot_count, rec_dev, 4, block_width))
+    width = traces.shape[3]
+    gathered = regroup(traces.reshape(2048, width)).reshape(32, 16, 4, width)
+    wavelet = finish(time_first(gathered))
     square = wavelet * wavelet
     planes_out = []
     for plane_index in range(PLANES):
@@ -121,17 +163,15 @@
     rate_float = rate_table.astype(jnp.float32)
     byte_limit = byte_target[0] * (wavelet.shape[0] * line_count * band_count)
 
-    def bisect_turn(turn_index, bounds):
-        bottom, ceiling = bounds
-        middle = (bottom + ceiling) // 2
-        chosen_rates = jnp.where(plane_gain >= slope_at(middle) * rate_float, rate_table, 0)
-        local_kept = jnp.sum(chosen_rates, dtype=jnp.int32)
-        total_kept = lax.psum(local_kept, ("line", "tm"))
-        within = total_kept <= byte_limit
-        return (jnp.where(within, bottom, middle), jnp.where(within, middle, ceiling))
-
-    bottom, ceiling = lax.fori_loop(0, BISECT, bisect_turn, (jnp.int32(0), jnp.int32(2**BISECT)))
-    slope_now = slope_at(ceiling)
+    trials = slope_at(jnp.arange(2**BISECT, dtype=jnp.int32))[:, None, None]
+    kept = jnp.sum(
+        jnp.where(plane_gain[None] >= trials * rate_float[None], rate_table[None], 0),
+        axis=(1, 2),
+        dtype=jnp.int32,
+    )
+    kept = lax.psum(kept, ("line", "tm"))
+    chosen = 1 + jnp.sum((kept[1:] > byte_limit).astype(jnp.int32))
+    slope_now = slope_at(chosen)
     rate_sums = jnp.sum(rate_table, axis=0).astype(jnp.float32)
     shrink_by = jnp.sqrt(slope_now * rate_sums / rate_scale)[:, None, None, None]
     return wavelet - jnp.clip(wavelet, -shrink_by, shrink_by)

time: 1360 us -> 237 us (0.17)
  blocking collectives: 1280 us -> 108 us
  Pallas kernels: 0 us -> 66.9 us
    psum x12 -> x1, blocking collectives: 1200 us -> 108 us  [body(): kept = lax.psum(kept, ('line', 'tm'))]
    all_to_all x1 -> x0, blocking collectives: 72 us -> none  [body(): lax.all_to_all(parted, 'line', split_axis=1, concat_axis=0, tiled=True)]
    pallas_call x0 -> x1, Pallas kernels: none -> 66.9 us  [regroup(): pl.pallas_call(regroup_kernel, out_shape=jax.ShapeDtypeStruct(rows.shape,...]
  transfers between devices with their start and end apart: 8 -> 8, of which waited for: 8 -> 8; matrix products, arithmetic and copies ran while one was open for 0% -> 1% of each run, Pallas kernels for 0% -> 0%
where the time goes in v1:
time: 237 us
  blocking collectives  108 us (46%)
  Pallas kernels  66.9 us (28%)
  waiting for transfers between devices  27.1 us (11%)
  starting transfers between devices  20.5 us (9%)
  local copies, waits for them, and re-layouts  8.76 us (4%)
  other arithmetic  4.22 us (2%)
    psum x1, blocking collectives, body(): kept = lax.psum(kept, ('line', 'tm'))  108 us
    pallas_call x1, Pallas kernels, regroup(): pl.pallas_call(regroup_kernel, out_shape=jax.ShapeDtypeStruct(rows.shape,...  66.9 us
    ppermute x8, waiting for transfers between devices, shifted(): lax.ppermute(value, axis, [(source, source + steps) for source in range(i...  27.1 us
    ppermute x8, starting transfers between devices, shifted(): lax.ppermute(value, axis, [(source, source + steps) for source in range(i...  20.5 us
  transfers between devices with their start and end apart: 8, of which 8 were waited for; matrix products, arithmetic and copies ran while one was open for 1% of the time, Pallas kernels for 0%

profile of v1, /device:TPU:1, one launch (start us, length us, event | category | flops | bytes accessed | tf_op | source)
XLA Modules:
  0.0 237.0 jit_solution(17977416680733990960)
XLA Ops:
  0.0 66.9 %regroup.1 = f32[2048,128]{1,0:T(8,128)} custom-call(f32[2048,128]{1,0:T(8,128)} %bitcast.100), custom_call_target="tpu_custom_call" | custom-call | tf_op jit(solution)/shard_map/regroup/pallas_call | solution.py:138
  66.9 3.7 %fusion.30 = (f32[32,16,1,128]{3,2,1,0:T(1,128)S(1)}, f32[32,16,1,128]{3,2,1,0:T(1,128)S(1)}, f32[32,16,1,128]{3,2,1,0:T(1,128)S(1)}, f32[32,16,1,128]{3,2,1,0:T(1,128)S(1)}) fusion(f32[32,16,4,128]{3,2,1,0:T(4,128)} %bitcast.88), kind=kLoop, calls=%fused_computation.69 | loop fusion | bytes 2097152 | tf_op jit(solution)/shard_map/slice | solution.py:50
  70.6 1.3 collective-permute-start
  72.1 7.9 %collective-permute-done = f32[32,16,1]{2,1,0:T(8,128)S(1)} collective-permute-done((f32[32,16,1]{2,1,0:T(8,128)S(1)}, f32[32,16,1]{2,1,0:T(8,128)S(1)}, u32[]{:S(2)}, u32[]{:S(2)}) %collective-permute-start) | collective-permute-done | bytes 2080 | tf_op jit(solution)/shard_map/ppermute | solution.py:20
  80.3 3.2 %collective-permute-start.1 = (f32[32,16,1]{2,1,0:T(8,128)S(1)}, f32[32,16,1]{2,1,0:T(8,128)S(1)}, u32[]{:S(2)}, u32[]{:S(2)}) collective-permute-start(f32[32,16,1]{2,1,0:T(8,128)S(1)} %slice.137), channel_id=1, source_target_pairs={{0,1},{1,2},{2,3},{4,5},{5,6},{6,7},{8,9},{9,10},{10,11},{12,13},{... | collective-permute-start | bytes 6152 | tf_op jit(solution)/shard_map/ppermute | solution.py:20
  83.9 3.9 %collective-permute-done.1 = f32[32,16,1]{2,1,0:T(8,128)S(1)} collective-permute-done((f32[32,16,1]{2,1,0:T(8,128)S(1)}, f32[32,16,1]{2,1,0:T(8,128)S(1)}, u32[]{:S(2)}, u32[]{:S(2)}) %collective-permute-start.1) | collective-permute-done | bytes 2080 | tf_op jit(solution)/shard_map/ppermute | solution.py:20
  89.2 4.1 %collective-permute-start.2 = (f32[32,1,4,128]{3,1,2,0:T(1,128)S(1)}, f32[32,1,4,128]{3,1,2,0:T(1,128)S(1)}, u32[]{:S(2)}, u32[]{:S(2)}) collective-permute-start(f32[32,1,4,128]{3,1,2,0:T(1,128)S(1)} %slice.141), channel_id=1, source_target_pairs={{4,0},{8,4},{12,8},{16,12},{20,16},{24,20},{28,24},{32,28},{36,32}... | collective-permute-start | bytes 196616 | tf_op jit(solution)/shard_map/ppermute | solution.py:20
  93.3 0.6 slice.108
  93.9 2.2 collective-permute-done.2
  96.4 1.9 collective-permute-start.3
  98.3 1.3 collective-permute-done.3
  99.9 0.6 copy.118
  100.6 1.3 collective-permute-start.4
  102.0 6.5 %collective-permute-done.4 = f32[32,8,1]{2,0,1:T(8,128)S(1)} collective-permute-done((f32[32,8,1]{2,0,1:T(8,128)S(1)}, f32[32,8,1]{2,0,1:T(8,128)S(1)}, u32[]{:S(2)}, u32[]{:S(2)}) %collective-permute-start.4) | collective-permute-done | bytes 1056 | tf_op jit(solution)/shard_map/ppermute | solution.py:20
  108.8 3.2 %collective-permute-start.5 = (f32[32,8,1]{2,0,1:T(8,128)S(1)}, f32[32,8,1]{2,0,1:T(8,128)S(1)}, u32[]{:S(2)}, u32[]{:S(2)}) collective-permute-start(f32[32,8,1]{2,0,1:T(8,128)S(1)} %slice.148), channel_id=1, source_target_pairs={{0,1},{1,2},{2,3},{4,5},{5,6},{6,7},{8,9},{9,10},{10,11},{12,13},{... | collective-permute-start | bytes 3080 | tf_op jit(solution)/shard_map/ppermute | solution.py:20
  111.9 1.9 collective-permute-done.5
  114.0 3.7 %collective-permute-start.6 = (f32[32,1,2,128]{3,0,2,1:T(8,128)S(1)}, f32[32,1,2,128]{3,0,2,1:T(8,128)S(1)}, u32[]{:S(2)}, u32[]{:S(2)}) collective-permute-start(f32[32,1,2,128]{3,0,2,1:T(8,128)S(1)} %slice.151), channel_id=1, source_target_pairs={{4,0},{8,4},{12,8},{16,12},{20,16},{24,20},{28,24},{32,28},{36,32}... | collective-permute-start | bytes 98312 | tf_op jit(solution)/shard_map/ppermute | solution.py:20
  117.8 2.9 %collective-permute-done.6 = f32[32,1,2,128]{3,0,2,1:T(8,128)S(1)} collective-permute-done((f32[32,1,2,128]{3,0,2,1:T(8,128)S(1)}, f32[32,1,2,128]{3,0,2,1:T(8,128)S(1)}, u32[]{:S(2)}, u32[]{:S(2)}) %collective-permute-start.6) | collective-permute-done | bytes 32800 | tf_op jit(solution)/shard_map/ppermute | solution.py:20
  120.7 1.9 collective-permute-start.7
  124.0 1.1 add_reduce_fusion
  125.2 0.7 select_reduce_fusion
  125.9 107.6 %psum.7 = s32[4096]{0:T(1024)S(1)} all-reduce(s32[4096]{0:T(1024)S(1)} %select_reduce_fusion), channel_id=1, replica_groups=mesh['line'=128,'tm'=4] {'line','tm'}, use_global_device_ids=true, to_apply=%region_9.10 | all-reduce | flops 4096 | bytes 32768 | tf_op jit(solution)/shard_map/psum | solution.py:172
  233.5 0.8 convert_reduce_fusion
  235.3 1.6 copy.126
  (46 shorter events, 4.4 us)
Async XLA Ops:
  70.6 9.4 %collective-permute-start = (f32[32,16,1]{2,1,0:T(8,128)S(1)}, f32[32,16,1]{2,1,0:T(8,128)S(1)}, u32[]{:S(2)}, u32[]{:S(2)}) collective-permute-start(f32[32,16,1]{2,1,0:T(8,128)S(1)} %bitcast.93), channel_id=1, source_target_pairs={{1,0},{2,1},{3,2},{5,4},{6,5},{7,6},{9,8},{10,9},{11,10},{13,12},{... | collective-permute-start | bytes 6152 | tf_op jit(solution)/shard_map/ppermute | solution.py:20
  80.3 7.6 %collective-permute-start.1 = (f32[32,16,1]{2,1,0:T(8,128)S(1)}, f32[32,16,1]{2,1,0:T(8,128)S(1)}, u32[]{:S(2)}, u32[]{:S(2)}) collective-permute-start(f32[32,16,1]{2,1,0:T(8,128)S(1)} %slice.137), channel_id=1, source_target_pairs={{0,1},{1,2},{2,3},{4,5},{5,6},{6,7},{8,9},{9,10},{10,11},{12,13},{... | collective-permute-start | bytes 6152 | tf_op jit(solution)/shard_map/ppermute | solution.py:20
  89.2 6.9 %collective-permute-start.2 = (f32[32,1,4,128]{3,1,2,0:T(1,128)S(1)}, f32[32,1,4,128]{3,1,2,0:T(1,128)S(1)}, u32[]{:S(2)}, u32[]{:S(2)}) collective-permute-start(f32[32,1,4,128]{3,1,2,0:T(1,128)S(1)} %slice.141), channel_id=1, source_target_pairs={{4,0},{8,4},{12,8},{16,12},{20,16},{24,20},{28,24},{32,28},{36,32}... | collective-permute-start | bytes 196616 | tf_op jit(solution)/shard_map/ppermute | solution.py:20
  96.4 3.2 %collective-permute-start.3 = (f32[32,1,4,128]{3,1,2,0:T(1,128)S(1)}, f32[32,1,4,128]{3,1,2,0:T(1,128)S(1)}, u32[]{:S(2)}, u32[]{:S(2)}) collective-permute-start(f32[32,1,4,128]{3,1,2,0:T(1,128)S(1)} %slice.142), channel_id=1, source_target_pairs={{0,4},{4,8},{8,12},{12,16},{16,20},{20,24},{24,28},{28,32},{32,36}... | collective-permute-start | bytes 196616 | tf_op jit(solution)/shard_map/ppermute | solution.py:20
  100.6 7.9 %collective-permute-start.4 = (f32[32,8,1]{2,0,1:T(8,128)S(1)}, f32[32,8,1]{2,0,1:T(8,128)S(1)}, u32[]{:S(2)}, u32[]{:S(2)}) collective-permute-start(f32[32,8,1]{2,0,1:T(8,128)S(1)} %bitcast.103), channel_id=1, source_target_pairs={{1,0},{2,1},{3,2},{5,4},{6,5},{7,6},{9,8},{10,9},{11,10},{13,12},{... | collective-permute-start | bytes 3080 | tf_op jit(solution)/shard_map/ppermute | solution.py:20
  108.7 9.0 %copy-start = (s32[1,1,8,32]{3,2,1,0:T(8,128)S(1)}, s32[1,1,8,32]{3,2,1,0:T(8,128)}, u32[]{:S(2)}) copy-start(s32[1,1,8,32]{3,2,1,0:T(8,128)} %param.4) | copy-start | bytes 3076
  108.8 5.1 %collective-permute-start.5 = (f32[32,8,1]{2,0,1:T(8,128)S(1)}, f32[32,8,1]{2,0,1:T(8,128)S(1)}, u32[]{:S(2)}, u32[]{:S(2)}) collective-permute-start(f32[32,8,1]{2,0,1:T(8,128)S(1)} %slice.148), channel_id=1, source_target_pairs={{0,1},{1,2},{2,3},{4,5},{5,6},{6,7},{8,9},{9,10},{10,11},{12,13},{... | collective-permute-start | bytes 3080 | tf_op jit(solution)/shard_map/ppermute | solution.py:20
  114.0 6.6 %collective-permute-start.6 = (f32[32,1,2,128]{3,0,2,1:T(8,128)S(1)}, f32[32,1,2,128]{3,0,2,1:T(8,128)S(1)}, u32[]{:S(2)}, u32[]{:S(2)}) collective-permute-start(f32[32,1,2,128]{3,0,2,1:T(8,128)S(1)} %slice.151), channel_id=1, source_target_pairs={{4,0},{8,4},{12,8},{16,12},{20,16},{24,20},{28,24},{32,28},{36,32}... | collective-permute-start | bytes 98312 | tf_op jit(solution)/shard_map/ppermute | solution.py:20
  120.7 3.1 %collective-permute-start.7 = (f32[32,1,2,128]{3,0,2,1:T(8,128)S(1)}, f32[32,1,2,128]{3,0,2,1:T(8,128)S(1)}, u32[]{:S(2)}, u32[]{:S(2)}) collective-permute-start(f32[32,1,2,128]{3,0,2,1:T(8,128)S(1)} %slice.152), channel_id=1, source_target_pairs={{0,4},{4,8},{8,12},{12,16},{16,20},{20,24},{24,28},{28,32},{32,36}... | collective-permute-start | bytes 98312 | tf_op jit(solution)/shard_map/ppermute | solution.py:20

commit v2 on v0

v2 whole, which is shorter than its diff:
```python
import jax
import jax.numpy as jnp
from jax import lax
from jax.experimental import pallas as pl
from jax.experimental.pallas import tpu as pltpu
from jax.sharding import PartitionSpec as P

PLANES = 8
BISECT = 12
LINES = 128
BANDS = 4
SHOTS = 32
GROUPS = 4
ROWS = 2048
SLOPE_ROWS = 2**BISECT // 128
MESH = pl.DeviceIdType.MESH

slope_floor = -12.0
slope_span = 32.0
rate_scale = 65536.0

PLANE_STEPS = sorted(
    [(dx, dc, dy) for dx in range(4) for dc in range(2) for dy in range(4)][1:],
    key=lambda s: (-(min(s[0], 4 - s[0]) + min(s[2], 4 - s[2])), s),
)
RING_STEPS = sorted(range(1, 16), key=lambda s: -min(s, 16 - s))


def remote(src, dst, ssem, rsem, line, tm):
    return pltpu.make_async_remote_copy(
        src_ref=src,
        dst_ref=dst,
        send_sem=ssem,
        recv_sem=rsem,
        device_id=(line, tm),
        device_id_type=MESH,
    )


def settle(ref, sem):
    pltpu.make_async_copy(ref, ref, sem).wait()


def detail(even_part, odd_part, ahead_even):
    return odd_part - 0.5 * (even_part + ahead_even)


def smooth(even_part, behind, details):
    return even_part + 0.25 * (behind + details)


def kernel(
    x_ref,
    rates_ref,
    target_ref,
    w_ref,
    shrink_ref,
    held,
    lifted,
    wave,
    time_send,
    time_recv,
    ahead_send,
    ahead_recv,
    back_send,
    back_recv,
    slopes,
    rate_cols,
    kept_acc,
    kept_rows,
    plane_slots,
    ring_row,
    ring_slots,
    count_row,
    count_slots,
    all_sems,
    time_sems,
    line_sems,
    tree_sems,
):
    line = lax.axis_index("line")
    tm = lax.axis_index("tm")
    z = line // 8
    x = (line // 2) % 4
    core = line % 2

    def plane_peer(step):
        dx, dc, dy = step
        peer_x = lax.rem(x + dx, 4)
        peer_core = lax.rem(core + dc, 2)
        return z * 8 + peer_x * 2 + peer_core, lax.rem(tm + dy, 4)

    def plane_index(line_at, tm_at):
        return (line_at % 8) * 4 + tm_at

    bar = pltpu.get_barrier_semaphore()

    @pl.loop(0, LINES - 1)
    def _(i):
        pl.semaphore_signal(
            bar, inc=1, device_id=(lax.rem(line + i + 1, LINES), tm), device_id_type=MESH
        )

    others = [s for s in PLANE_STEPS if s[2]]
    for step in others:
        pl.semaphore_signal(bar, inc=1, device_id=plane_peer(step), device_id_type=MESH)
    pl.semaphore_wait(bar, LINES - 1 + len(others))

    mine = held.at[pl.ds(pl.multiple_of(line * 16, 16), 16)]

    @pl.loop(0, LINES - 1)
    def _(i):
        to = lax.rem(line + i + 1, LINES)
        remote(
            x_ref.at[pl.ds(pl.multiple_of(to * 16, 16), 16)],
            mine,
            all_sems.at[0],
            all_sems.at[1],
            to,
            tm,
        ).start()

    own = pltpu.make_async_copy(
        x_ref.at[pl.ds(pl.multiple_of(line * 16, 16), 16)], mine, all_sems.at[2]
    )
    own.start()

    lane = lax.broadcasted_iota(jnp.int32, (8, 128), 1)
    sub = lax.broadcasted_iota(jnp.int32, (8, 128), 0)
    for row in range(SLOPE_ROWS):
        grid_index = (lane + row * 128).astype(jnp.float32)
        slopes[row] = jnp.exp2(slope_floor + grid_index * (slope_span / 2**BISECT))
        kept_acc[row] = jnp.zeros((8, 128), jnp.float32)
    for group in range(GROUPS):
        total = jnp.zeros((8, 128), jnp.float32)
        for plane in range(PLANES):
            rate_row = rates_ref[plane : plane + 1, :].astype(jnp.float32)
            picked = jnp.where(
                lane[:, :SHOTS] == sub[:, :SHOTS] + group * 8,
                jnp.broadcast_to(rate_row, (8, SHOTS)),
                0.0,
            )
            column = jnp.broadcast_to(jnp.sum(picked, axis=1, keepdims=True), (8, 128))
            rate_cols[plane, group * 8 : group * 8 + 8] = column
            total = total + column
        rate_cols[PLANES, group * 8 : group * 8 + 8] = total

    own.wait()
    most = held.at[pl.ds(0, ROWS - 16)]
    settle(most, all_sems.at[1])

    def phases(group, r):
        return [held[pl.ds(group * 512 + r * 4 + q, 8, stride=64), :] for q in range(4)]

    def span(group):
        return pl.ds(pl.multiple_of(group * 8, 8), 8)

    up = lax.rem(tm + 1, 4)
    down = lax.rem(tm + 3, 4)

    def time_copy(way, group):
        to = up if way == 0 else down
        return remote(
            time_send.at[way, span(group)],
            time_recv.at[way, span(group)],
            time_sems.at[0, way, group],
            time_sems.at[1, way, group],
            line,
            to,
        )

    @pl.loop(0, GROUPS)
    def _(group):
        to_next = jnp.zeros((8, 128), jnp.float32)
        to_prev = jnp.zeros((8, 128), jnp.float32)
        for r in range(16):
            p0, p1, p2, p3 = phases(group, r)
            d1 = detail(p0, p1, p2)
            d3 = detail(p2, p3, pltpu.roll(p0, 127, 1))
            s0 = smooth(p0, pltpu.roll(d3, 1, 1), d1)
            rim_detail = p3 - 0.5 * p2
            rim_second = p2 + 0.25 * d1 - 0.5 * s0
            rim_smooth = p0 + 0.25 * d1
            at = 2 * r
            to_next = jnp.where(lane == at, pltpu.roll(rim_detail, at + 1, 1), to_next)
            to_next = jnp.where(lane == at + 1, pltpu.roll(rim_second, at + 2, 1), to_next)
            to_prev = jnp.where(lane == at, pltpu.roll(p0, at, 1) if at else p0, to_prev)
            to_prev = jnp.where(lane == at + 1, pltpu.roll(rim_smooth, at + 1, 1), to_prev)
        time_send[0, span(group)] = to_next
        time_send[1, span(group)] = to_prev
        time_copy(0, group).start()
        time_copy(1, group).start()

    has_prev_band = jnp.where(tm > 0, 1.0, 0.0)
    has_next_band = jnp.where(tm < BANDS - 1, 1.0, 0.0)
    has_prev_line = jnp.where(line > 0, 1.0, 0.0)
    has_next_line = jnp.where(line < LINES - 1, 1.0, 0.0)
    line_up = lax.rem(line + 1, LINES)
    line_down = lax.rem(line + LINES - 1, LINES)

    def line_copy(way, group):
        if way == 0:
            return remote(
                ahead_send.at[:, span(group)],
                ahead_recv.at[:, span(group)],
                line_sems.at[0, 0, group],
                line_sems.at[1, 0, group],
                line_down,
                tm,
            )
        return remote(
            back_send.at[:, span(group)],
            back_recv.at[:, span(group)],
            line_sems.at[0, 1, group],
            line_sems.at[1, 1, group],
            line_up,
            tm,
        )

    @pl.loop(0, GROUPS)
    def _(group):
        time_copy(0, group).wait_recv()
        time_copy(1, group).wait_recv()
        from_prev = time_recv[0, span(group)]
        from_next = time_recv[1, span(group)]
        low = []
        high = []
        one = []
        three = []
        for r in range(16):
            at = 2 * r
            p0, p1, p2, p3 = phases(group, r)
            d1 = detail(p0, p1, p2)
            ahead = jnp.where(
                lane == 127,
                pltpu.roll(from_next, 127 - at, 1) * has_next_band,
                pltpu.roll(p0, 127, 1),
            )
            d3 = detail(p2, p3, ahead)
            rim = pltpu.roll(from_prev, 128 - at, 1) if at else from_prev
            d3_prev = (rim - 0.5 * p0) * has_prev_band
            s0 = smooth(p0, jnp.where(lane == 0, d3_prev, pltpu.roll(d3, 1, 1)), d1)
            s2 = smooth(p2, d1, d3)
            next_s0 = (pltpu.roll(from_next, 126 - at, 1) + 0.25 * d3) * has_next_band
            second = detail(s0, s2, jnp.where(lane == 127, next_s0, pltpu.roll(s0, 127, 1)))
            rim = pltpu.roll(from_prev, 127 - at, 1)
            second_prev = (rim + 0.25 * d3_prev - 0.5 * s0) * has_prev_band
            first = smooth(
                s0, jnp.where(lane == 0, second_prev, pltpu.roll(second, 1, 1)), second
            )
            for slot, value in enumerate((s0, d1, s2, d3, first, second)):
                lifted[slot, r, span(group)] = value
            if r == 0:
                for slot, value in enumerate((s0, d1, s2, d3, first, second)):
                    ahead_send[slot, span(group)] = value
            one.append(d1)
            three.append(d3)
            low.append(first)
            high.append(second)
        for slot, value in enumerate((low, high)):
            ahead_send[6 + slot, span(group)] = value[0] + 0.25 * detail(value[0], value[1], value[2])
            d5 = detail(value[10], value[11], value[12])
            d6 = detail(value[12], value[13], value[14])
            s6 = smooth(value[12], d5, d6)
            back_send[4 + slot, span(group)] = value[14] + 0.25 * d6 - 0.5 * s6
        for slot, value in enumerate((one, three, low, high)):
            back_send[slot, span(group)] = value[15] - 0.5 * value[14]
        line_copy(0, group).start()
        line_copy(1, group).start()

    @pl.loop(0, GROUPS)
    def _(group):
        line_copy(0, group).wait_recv()
        line_copy(1, group).wait_recv()
        gains = [jnp.zeros((8, 128), jnp.float32) for _ in range(PLANES)]

        def put(r, q, value):
            wave[pl.ds(group * 512 + r * 4 + q, 8, stride=64), :] = value
            square = value * value
            capped = [jnp.minimum(square, 4.0 ** (4 - p)) for p in range(PLANES + 1)]
            for p in range(PLANES):
                gains[p] = gains[p] + (capped[p] - capped[p + 1])

        def lift(slot, back_slot, put_odd):
            values = [lifted[slot, r, span(group)] for r in range(16)]
            values.append(ahead_recv[slot, span(group)] * has_next_line)
            details = [
                detail(values[2 * i], values[2 * i + 1], values[2 * i + 2]) for i in range(8)
            ]
            if put_odd is not None:
                for i in range(8):
                    put(2 * i + 1, put_odd, details[i])
            if back_slot is None:
                return None
            behind = (back_recv[back_slot, span(group)] - 0.5 * values[0]) * has_prev_line
            chain = [behind] + details
            smooths = [smooth(values[2 * i], chain[i], chain[i + 1]) for i in range(8)]
            return smooths, behind, details[7]

        for q in (0, 2):
            lift(q, None, q)
        for q, back_slot in ((1, 0), (3, 1)):
            smooths, _, _ = lift(q, back_slot, q)
            for i in range(8):
                put(2 * i, q, smooths[i])
        for k, q in ((0, 0), (1, 2)):
            smooths, behind, last = lift(4 + k, 2 + k, None)
            smooths.append((ahead_recv[6 + k, span(group)] + 0.25 * last) * has_next_line)
            details = [
                detail(smooths[2 * i], smooths[2 * i + 1], smooths[2 * i + 2]) for i in range(4)
            ]
            behind_two = (
                back_recv[4 + k, span(group)] + 0.25 * behind - 0.5 * smooths[0]
            ) * has_prev_line
            chain = [behind_two] + details
            for i in range(4):
                put(4 * i, q, smooth(smooths[2 * i], chain[i], chain[i + 1]))
                put(4 * i + 2, q, details[i])

        sums = [
            jnp.broadcast_to(jnp.sum(gains[p], axis=1, keepdims=True), (8, 128))
            for p in range(PLANES)
        ]
        rates = [rate_cols[p, span(group)] for p in range(PLANES)]

        @pl.loop(0, SLOPE_ROWS, unroll=4)
        def _(row):
            slope = slopes[row]
            total = kept_acc[row]
            for p in range(PLANES):
                total = total + jnp.where(sums[p] >= slope * rates[p], rates[p], 0.0)
            kept_acc[row] = total

    out = pltpu.make_async_copy(wave, w_ref, all_sems.at[2])
    out.start()

    kept_rows[...] = jnp.sum(kept_acc[...], axis=1).astype(jnp.int32)
    place = plane_index(line, tm)

    def row_of(ref, index):
        return ref.at[pl.ds(index, 1)]

    for step in PLANE_STEPS:
        to_line, to_tm = plane_peer(step)
        remote(
            row_of(kept_rows, plane_index(to_line, to_tm)),
            row_of(plane_slots, place),
            tree_sems.at[0, 0],
            tree_sems.at[1, 0],
            to_line,
            to_tm,
        ).start()
    plane_slots[pl.ds(place, 1)] = kept_rows[pl.ds(place, 1)]
    settle(plane_slots.at[pl.ds(0, 31)], tree_sems.at[1, 0])
    ring_row[...] = jnp.sum(plane_slots[...], axis=0, keepdims=True)

    for step in RING_STEPS:
        remote(
            ring_row,
            row_of(ring_slots, z),
            tree_sems.at[0, 1],
            tree_sems.at[1, 1],
            lax.rem(line + step * 8, LINES),
            tm,
        ).start()
    ring_slots[pl.ds(z, 1)] = ring_row[...]
    settle(ring_slots.at[pl.ds(0, 15)], tree_sems.at[1, 1])
    kept = jnp.sum(ring_slots[...], axis=0, keepdims=True)
    limit = target_ref[0] * (SHOTS * LINES * BANDS)
    grid_row = lax.broadcasted_iota(jnp.int32, (1, 128), 1) + place * 128
    above = jnp.where((kept > limit) & (grid_row > 0), 1.0, 0.0)
    count_row[...] = jnp.broadcast_to(jnp.sum(above, axis=1, keepdims=True), (1, 128))

    for step in PLANE_STEPS:
        to_line, to_tm = plane_peer(step)
        remote(
            count_row,
            row_of(count_slots, place),
            tree_sems.at[0, 2],
            tree_sems.at[1, 2],
            to_line,
            to_tm,
        ).start()
    count_slots[pl.ds(place, 1)] = count_row[...]
    settle(count_slots.at[pl.ds(0, 31)], tree_sems.at[1, 2])
    chosen = 1.0 + jnp.sum(count_slots[...], axis=0, keepdims=True)
    slope_now = jnp.exp2(slope_floor + chosen * (slope_span / 2**BISECT))
    shrink_ref[...] = jnp.sqrt(slope_now * rate_cols[PLANES] / rate_scale)

    out.wait()
    settle(most, all_sems.at[0])

    @pl.loop(0, GROUPS)
    def _(group):
        for way in range(2):
            time_copy(way, group).wait_send()
            line_copy(way, group).wait_send()

    settle(plane_slots.at[pl.ds(0, 31)], tree_sems.at[0, 0])
    settle(ring_slots.at[pl.ds(0, 15)], tree_sems.at[0, 1])
    settle(count_slots.at[pl.ds(0, 31)], tree_sems.at[0, 2])


def transform(rows, rates, byte_target):
    vmem = pl.BlockSpec(memory_space=pltpu.VMEM)
    hbm = pl.BlockSpec(memory_space=pl.ANY)
    f32 = jnp.float32
    return pl.pallas_call(
        kernel,
        out_shape=[
            jax.ShapeDtypeStruct((ROWS, 128), f32),
            jax.ShapeDtypeStruct((SHOTS, 128), f32),
        ],
        in_specs=[hbm, vmem, pl.BlockSpec(memory_space=pltpu.SMEM)],
        out_specs=[hbm, vmem],
        scratch_shapes=[
            pltpu.VMEM((ROWS, 128), f32),
            pltpu.VMEM((6, 16, SHOTS, 128), f32),
            pltpu.VMEM((ROWS, 128), f32),
            pltpu.VMEM((2, SHOTS, 128), f32),
            pltpu.VMEM((2, SHOTS, 128), f32),
            pltpu.VMEM((8, SHOTS, 128), f32),
            pltpu.VMEM((8, SHOTS, 128), f32),
            pltpu.VMEM((6, SHOTS, 128), f32),
            pltpu.VMEM((6, SHOTS, 128), f32),
            pltpu.VMEM((SLOPE_ROWS, 8, 128), f32),
            pltpu.VMEM((PLANES + 1, SHOTS, 128), f32),
            pltpu.VMEM((SLOPE_ROWS, 8, 128), f32),
            pltpu.VMEM((SLOPE_ROWS, 128), jnp.int32),
            pltpu.VMEM((SLOPE_ROWS, 128), jnp.int32),
            pltpu.VMEM((1, 128), jnp.int32),
            pltpu.VMEM((16, 128), jnp.int32),
            pltpu.VMEM((1, 128), f32),
            pltpu.VMEM((32, 128), f32),
            pltpu.SemaphoreType.DMA((3,)),
            pltpu.SemaphoreType.DMA((2, 2, GROUPS)),
            pltpu.SemaphoreType.DMA((2, 2, GROUPS)),
            pltpu.SemaphoreType.DMA((2, 3)),
        ],
        compiler_params=pltpu.CompilerParams(
            collective_id=1, has_side_effects=True, vmem_limit_bytes=24 * 2**20
        ),
        name="transform",
    )(rows, rates, byte_target)


def body(traces, rates, byte_target):
    width = traces.shape[3]
    rows = traces.reshape(ROWS, width)
    wave, shrink = transform(rows, rates.reshape(PLANES, SHOTS), byte_target)
    wavelet = wave.reshape(SHOTS, 16, 4, width)
    shrink_by = shrink[:, None, None, :]
    return wavelet - jnp.clip(wavelet, -shrink_by, shrink_by)


def solution(mesh):
    return jax.shard_map(
        body,
        mesh=mesh,
        in_specs=(P("line", None, None, "tm"), P("line", "tm", None, None), P()),
        out_specs=P(None, "line", None, "tm"),
        check_vma=False,
    )
```

time: 1360 us -> 101 us (0.07)
  blocking collectives: 1280 us -> 0 us
  Pallas kernels: 0 us -> 97.5 us
  waiting for transfers between devices: 28.1 us -> 0 us
  starting transfers between devices: 22.8 us -> 0 us
    psum x12 -> x0, blocking collectives: 1200 us -> none  [bisect_turn(): total_kept = lax.psum(local_kept, ('line', 'tm'))]
    pallas_call x0 -> x1, Pallas kernels: none -> 97.5 us  [transform(): pl.pallas_call(kernel, out_shape=[jax.ShapeDtypeStruct((ROWS, 128), f32),...]
    all_to_all x1 -> x0, blocking collectives: 72 us -> none  [body(): lax.all_to_all(parted, 'line', split_axis=1, concat_axis=0, tiled=True)]
    ppermute x8 -> x0, waiting for transfers between devices: 28.1 us -> none  [shifted(): lax.ppermute(value, axis, [(source, source + steps) for source in range(i...]
    ppermute x8 -> x0, starting transfers between devices: 22.8 us -> none  [shifted(): lax.ppermute(value, axis, [(source, source + steps) for source in range(i...]
  transfers between devices with their start and end apart: 8 -> 0, of which waited for: 8 -> 0; matrix products, arithmetic and copies ran while one was open for 0% -> 0% of each run, Pallas kernels for 0% -> 0%
where the time goes in v2:
time: 101 us
  Pallas kernels  97.5 us (97%)
  other arithmetic  1.32 us (1%)
  local copies, waits for them, and re-layouts  1.25 us (1%)
    pallas_call x1, Pallas kernels, transform(): pl.pallas_call(kernel, out_shape=[jax.ShapeDtypeStruct((ROWS, 128), f32),...  97.5 us

profile of v2, /device:TPU:1, one launch (start us, length us, event | category | flops | bytes accessed | tf_op | source)
XLA Modules:
  0.0 100.8 jit_solution(3806689920965921211)
XLA Ops:
  0.0 0.0 copy-start.1
  0.7 0.0 copy-done.1
  0.7 0.0 copy-start
  0.7 1.2 %copy-done = f32[1,512,4,128]{3,2,1,0:T(4,128)S(1)} copy-done((f32[1,512,4,128]{3,2,1,0:T(4,128)S(1)}, f32[1,512,4,128]{3,2,1,0:T(4,128)}, u32[]{:S(2)}) %copy-start) | copy-done | bytes 1048600
  1.9 97.5 %transform.1 = (f32[2048,128]{1,0:T(8,128)S(1)}, f32[32,128]{1,0:T(8,128)S(1)}) custom-call(f32[2048,128]{1,0:T(8,128)S(1)} %bitcast.3, s32[8,32]{1,0:T(8,128)S(1)} %bitcast.5, s32[1]{0:T(128)S(6)} %copy.4.target_ref), custom_call_target="tpu_custom_call" | custom-call | tf_op jit(solution)/shard_map/transform/pallas_call | solution.py:408
  99.5 1.3 %minimum_subtract_fusion = f32[32,16,4,128]{3,2,1,0:T(4,128)} fusion(f32[32,16,4,128]{3,2,1,0:T(4,128)S(1)} %bitcast.4, f32[32,128]{1,0:T(8,128)S(1)} %neg.4, f32[32,128]{1,0:T(8,128)S(1)} %get-tuple-element.8), kind=kLoop, calls=%fused_computation | loop fusion | flops 786432 | bytes 2129920 | tf_op jit(solution)/shard_map/sub | solution.py:453
  (1 shorter events, 0.0 us)
Async XLA Ops:
  0.0 0.7 copy-start.1
  0.7 1.2 %copy-start = (f32[1,512,4,128]{3,2,1,0:T(4,128)S(1)}, f32[1,512,4,128]{3,2,1,0:T(4,128)}, u32[]{:S(2)}) copy-start(f32[1,512,4,128]{3,2,1,0:T(4,128)} %param.3) | copy-start | bytes 3145732

commit v3 on v2

--- a/solution.py
+++ b/solution.py
@@ -12,6 +12,7 @@
 SHOTS = 32
 GROUPS = 4
 ROWS = 2048
+FIRST = 17
 SLOPE_ROWS = 2**BISECT // 128
 MESH = pl.DeviceIdType.MESH
 
@@ -55,15 +56,21 @@
     target_ref,
     w_ref,
     shrink_ref,
+    local,
     held,
     lifted,
     wave,
-    time_send,
-    time_recv,
+    rim_own,
+    rim_bands,
+    rim_merged,
+    rim_plane,
+    rim_ring,
+    rims,
     ahead_send,
     ahead_recv,
     back_send,
     back_recv,
+    rate_table,
     slopes,
     rate_cols,
     kept_acc,
@@ -73,8 +80,10 @@
     ring_slots,
     count_row,
     count_slots,
-    all_sems,
-    time_sems,
+    own_sems,
+    send_sem,
+    arrive_sems,
+    rim_sems,
     line_sems,
     tree_sems,
 ):
@@ -83,6 +92,7 @@
     z = line // 8
     x = (line // 2) % 4
     core = line % 2
+    spot = line % 8
 
     def plane_peer(step):
         dx, dc, dy = step
@@ -93,40 +103,110 @@
     def plane_index(line_at, tm_at):
         return (line_at % 8) * 4 + tm_at
 
+    def span(group):
+        return pl.ds(pl.multiple_of(group * 8, 8), 8)
+
+    def row_of(ref, index):
+        return ref.at[pl.ds(index, 1)]
+
+    fetch = pltpu.make_async_copy(x_ref, local, own_sems.at[0])
+    fetch.start()
+    fetch_rates = pltpu.make_async_copy(rates_ref, rate_table, own_sems.at[1])
+    fetch_rates.start()
+
+    up = lax.rem(tm + 1, 4)
+    down = lax.rem(tm + 3, 4)
     bar = pltpu.get_barrier_semaphore()
 
-    @pl.loop(0, LINES - 1)
+    @pl.loop(0, 15)
     def _(i):
+        near = 8 - (i + 1) // 2
+        step = jnp.where(i % 2 == 0, near, 16 - near)
+        plane = lax.rem(z + step, 16) * 8
+        for k in range(8):
+            pl.semaphore_signal(bar, inc=1, device_id=(plane + k, tm), device_id_type=MESH)
+
+    for k in range(1, 8):
         pl.semaphore_signal(
-            bar, inc=1, device_id=(lax.rem(line + i + 1, LINES), tm), device_id_type=MESH
+            bar, inc=1, device_id=(z * 8 + lax.rem(spot + k, 8), tm), device_id_type=MESH
         )
-
-    others = [s for s in PLANE_STEPS if s[2]]
-    for step in others:
-        pl.semaphore_signal(bar, inc=1, device_id=plane_peer(step), device_id_type=MESH)
-    pl.semaphore_wait(bar, LINES - 1 + len(others))
+    for to in (up, down):
+        pl.semaphore_signal(bar, inc=1, device_id=(line, to), device_id_type=MESH)
+
+    lane = lax.broadcasted_iota(jnp.int32, (8, 128), 1)
+    sub = lax.broadcasted_iota(jnp.int32, (8, 128), 0)
+    fetch.wait()
+
+    @pl.loop(0, 16)
+    def _(plane):
+        total = jnp.zeros((8, 128), jnp.float32)
+        for block in range(4):
+            p0, p1, p2, p3 = [
+                local[pl.ds(plane * 128 + block * 32 + q, 8, stride=4), :] for q in range(4)
+            ]
+            d1 = detail(p0, p1, p2)
+            d3 = detail(p2, p3, pltpu.roll(p0, 127, 1))
+            s0 = smooth(p0, pltpu.roll(d3, 1, 1), d1)
+            rim_detail = p3 - 0.5 * p2
+            rim_second = p2 + 0.25 * d1 - 0.5 * s0
+            rim_smooth = p0 + 0.25 * d1
+            columns = (
+                rim_detail[:, 127:128],
+                rim_second[:, 127:128],
+                p0[:, 0:1],
+                rim_smooth[:, 0:1],
+            )
+            for v, column in enumerate(columns):
+                at = (sub + block * 8) * 4 + v
+                total = jnp.where(lane == at, jnp.broadcast_to(column, (8, 128)), total)
+        rim_own[pl.ds(plane, 1), :] = jnp.sum(total, axis=0, keepdims=True)
+
+    pl.semaphore_wait(bar, LINES + 1)
+
+    band_up = remote(rim_own, rim_bands.at[0], rim_sems.at[0, 0], rim_sems.at[1, 0], line, up)
+    band_down = remote(rim_own, rim_bands.at[1], rim_sems.at[0, 1], rim_sems.at[1, 1], line, down)
+    band_up.start()
+    band_down.start()
 
     mine = held.at[pl.ds(pl.multiple_of(line * 16, 16), 16)]
-
-    @pl.loop(0, LINES - 1)
-    def _(i):
-        to = lax.rem(line + i + 1, LINES)
+    pltpu.make_async_copy(
+        x_ref.at[pl.ds(pl.multiple_of(line * 16, 16), 16)], mine, arrive_sems.at[z // 4]
+    ).start()
+
+    def scatter(first, last):
+        @pl.loop(first, last)
+        def _(i):
+            to = lax.rem(line + i, LINES)
+            remote(
+                x_ref.at[pl.ds(pl.multiple_of(to * 16, 16), 16)],
+                mine,
+                send_sem.at[0],
+                arrive_sems.at[z // 4],
+                to,
+                tm,
+            ).start()
+
+    scatter(1, FIRST)
+
+    band_up.wait_recv()
+    band_down.wait_recv()
+    lane16 = lax.broadcasted_iota(jnp.int32, (16, 128), 1)
+    rim_merged[...] = jnp.where(lane16 % 4 < 2, rim_bands[0], rim_bands[1])
+    for step in RING_STEPS:
+        to = lax.rem(z + step, 16)
         remote(
-            x_ref.at[pl.ds(pl.multiple_of(to * 16, 16), 16)],
-            mine,
-            all_sems.at[0],
-            all_sems.at[1],
-            to,
+            row_of(rim_merged, to),
+            row_of(rim_ring, z),
+            rim_sems.at[0, 3],
+            rim_sems.at[1, 3],
+            to * 8 + spot,
             tm,
         ).start()
-
-    own = pltpu.make_async_copy(
-        x_ref.at[pl.ds(pl.multiple_of(line * 16, 16), 16)], mine, all_sems.at[2]
-    )
-    own.start()
-
-    lane = lax.broadcasted_iota(jnp.int32, (8, 128), 1)
-    sub = lax.broadcasted_iota(jnp.int32, (8, 128), 0)
+    rim_ring[pl.ds(z, 1), :] = rim_merged[pl.ds(z, 1), :]
+
+    scatter(FIRST, LINES)
+
+    fetch_rates.wait()
     for row in range(SLOPE_ROWS):
         grid_index = (lane + row * 128).astype(jnp.float32)
         slopes[row] = jnp.exp2(slope_floor + grid_index * (slope_span / 2**BISECT))
@@ -134,7 +214,7 @@
     for group in range(GROUPS):
         total = jnp.zeros((8, 128), jnp.float32)
         for plane in range(PLANES):
-            rate_row = rates_ref[plane : plane + 1, :].astype(jnp.float32)
+            rate_row = rate_table[plane : plane + 1, :].astype(jnp.float32)
             picked = jnp.where(
                 lane[:, :SHOTS] == sub[:, :SHOTS] + group * 8,
                 jnp.broadcast_to(rate_row, (8, SHOTS)),
@@ -145,51 +225,25 @@
             total = total + column
         rate_cols[PLANES, group * 8 : group * 8 + 8] = total
 
-    own.wait()
-    most = held.at[pl.ds(0, ROWS - 16)]
-    settle(most, all_sems.at[1])
-
-    def phases(group, r):
-        return [held[pl.ds(group * 512 + r * 4 + q, 8, stride=64), :] for q in range(4)]
-
-    def span(group):
-        return pl.ds(pl.multiple_of(group * 8, 8), 8)
-
-    up = lax.rem(tm + 1, 4)
-    down = lax.rem(tm + 3, 4)
-
-    def time_copy(way, group):
-        to = up if way == 0 else down
-        return remote(
-            time_send.at[way, span(group)],
-            time_recv.at[way, span(group)],
-            time_sems.at[0, way, group],
-            time_sems.at[1, way, group],
-            line,
-            to,
-        )
-
-    @pl.loop(0, GROUPS)
-    def _(group):
-        to_next = jnp.zeros((8, 128), jnp.float32)
-        to_prev = jnp.zeros((8, 128), jnp.float32)
-        for r in range(16):
-            p0, p1, p2, p3 = phases(group, r)
-            d1 = detail(p0, p1, p2)
-            d3 = detail(p2, p3, pltpu.roll(p0, 127, 1))
-            s0 = smooth(p0, pltpu.roll(d3, 1, 1), d1)
-            rim_detail = p3 - 0.5 * p2
-            rim_second = p2 + 0.25 * d1 - 0.5 * s0
-            rim_smooth = p0 + 0.25 * d1
-            at = 2 * r
-            to_next = jnp.where(lane == at, pltpu.roll(rim_detail, at + 1, 1), to_next)
-            to_next = jnp.where(lane == at + 1, pltpu.roll(rim_second, at + 2, 1), to_next)
-            to_prev = jnp.where(lane == at, pltpu.roll(p0, at, 1) if at else p0, to_prev)
-            to_prev = jnp.where(lane == at + 1, pltpu.roll(rim_smooth, at + 1, 1), to_prev)
-        time_send[0, span(group)] = to_next
-        time_send[1, span(group)] = to_prev
-        time_copy(0, group).start()
-        time_copy(1, group).start()
+    settle(rim_ring.at[pl.ds(0, 15)], rim_sems.at[1, 3])
+    for k in range(1, 8):
+        remote(
+            rim_ring,
+            rim_plane.at[spot],
+            rim_sems.at[0, 2],
+            rim_sems.at[1, 2],
+            z * 8 + lax.rem(spot + k, 8),
+            tm,
+        ).start()
+    rim_plane[spot] = rim_ring[...]
+    settle(rim_plane.at[pl.ds(0, 7)], rim_sems.at[1, 2])
+    packed = jnp.zeros((16, 128), jnp.float32)
+    for k in range(8):
+        turned = pltpu.roll(rim_plane[k], lax.rem((k + 8 - spot) * 16, 128), 1)
+        packed = jnp.where(lane16 // 16 == k, turned, packed)
+
+    rims[pl.ds(0, 16, stride=2), :] = packed
+    rims[pl.ds(1, 16, stride=2), :] = pltpu.roll(packed, 64, 1)
 
     has_prev_band = jnp.where(tm > 0, 1.0, 0.0)
     has_next_band = jnp.where(tm < BANDS - 1, 1.0, 0.0)
@@ -217,34 +271,38 @@
             tm,
         )
 
+    def group_at(turn):
+        return lax.rem(z // 4 + 3 - turn + GROUPS, GROUPS)
+
     @pl.loop(0, GROUPS)
-    def _(group):
-        time_copy(0, group).wait_recv()
-        time_copy(1, group).wait_recv()
-        from_prev = time_recv[0, span(group)]
-        from_next = time_recv[1, span(group)]
+    def _(turn):
+        group = group_at(turn)
+        settle(held.at[pl.ds(0, ROWS // GROUPS)], arrive_sems.at[group])
+        rim = rims[span(group)]
         low = []
         high = []
         one = []
         three = []
         for r in range(16):
-            at = 2 * r
-            p0, p1, p2, p3 = phases(group, r)
+            at = 4 * r
+            p0, p1, p2, p3 = [
+                held[pl.ds(group * 512 + r * 4 + q, 8, stride=64), :] for q in range(4)
+            ]
             d1 = detail(p0, p1, p2)
             ahead = jnp.where(
                 lane == 127,
-                pltpu.roll(from_next, 127 - at, 1) * has_next_band,
+                pltpu.roll(rim, 125 - at, 1) * has_next_band,
                 pltpu.roll(p0, 127, 1),
             )
             d3 = detail(p2, p3, ahead)
-            rim = pltpu.roll(from_prev, 128 - at, 1) if at else from_prev
-            d3_prev = (rim - 0.5 * p0) * has_prev_band
+            rim_detail = pltpu.roll(rim, 128 - at, 1) if at else rim
+            d3_prev = (rim_detail - 0.5 * p0) * has_prev_band
             s0 = smooth(p0, jnp.where(lane == 0, d3_prev, pltpu.roll(d3, 1, 1)), d1)
             s2 = smooth(p2, d1, d3)
-            next_s0 = (pltpu.roll(from_next, 126 - at, 1) + 0.25 * d3) * has_next_band
+            next_s0 = (pltpu.roll(rim, 124 - at, 1) + 0.25 * d3) * has_next_band
             second = detail(s0, s2, jnp.where(lane == 127, next_s0, pltpu.roll(s0, 127, 1)))
-            rim = pltpu.roll(from_prev, 127 - at, 1)
-            second_prev = (rim + 0.25 * d3_prev - 0.5 * s0) * has_prev_band
+            rim_second = pltpu.roll(rim, 127 - at, 1)
+            second_prev = (rim_second + 0.25 * d3_prev - 0.5 * s0) * has_prev_band
             first = smooth(
                 s0, jnp.where(lane == 0, second_prev, pltpu.roll(second, 1, 1)), second
             )
@@ -269,7 +327,8 @@
         line_copy(1, group).start()
 
     @pl.loop(0, GROUPS)
-    def _(group):
+    def _(turn):
+        group = group_at(turn)
         line_copy(0, group).wait_recv()
         line_copy(1, group).wait_recv()
         gains = [jnp.zeros((8, 128), jnp.float32) for _ in range(PLANES)]
@@ -331,14 +390,11 @@
                 total = total + jnp.where(sums[p] >= slope * rates[p], rates[p], 0.0)
             kept_acc[row] = total
 
-    out = pltpu.make_async_copy(wave, w_ref, all_sems.at[2])
+    out = pltpu.make_async_copy(wave, w_ref, own_sems.at[0])
     out.start()
 
     kept_rows[...] = jnp.sum(kept_acc[...], axis=1).astype(jnp.int32)
     place = plane_index(line, tm)
-
-    def row_of(ref, index):
-        return ref.at[pl.ds(index, 1)]
 
     for step in PLANE_STEPS:
         to_line, to_tm = plane_peer(step)
@@ -388,12 +444,15 @@
     shrink_ref[...] = jnp.sqrt(slope_now * rate_cols[PLANES] / rate_scale)
 
     out.wait()
-    settle(most, all_sems.at[0])
+    settle(held.at[pl.ds(0, ROWS - 16)], send_sem.at[0])
+    band_up.wait_send()
+    band_down.wait_send()
+    settle(rim_plane.at[pl.ds(0, 7)], rim_sems.at[0, 2])
+    settle(rim_ring.at[pl.ds(0, 15)], rim_sems.at[0, 3])
 
     @pl.loop(0, GROUPS)
     def _(group):
         for way in range(2):
-            time_copy(way, group).wait_send()
             line_copy(way, group).wait_send()
 
     settle(plane_slots.at[pl.ds(0, 31)], tree_sems.at[0, 0])
@@ -404,6 +463,7 @@
 def transform(rows, rates, byte_target):
     vmem = pl.BlockSpec(memory_space=pltpu.VMEM)
     hbm = pl.BlockSpec(memory_space=pl.ANY)
+    rows, rates = [pltpu.with_memory_space_constraint(a, pltpu.HBM) for a in (rows, rates)]
     f32 = jnp.float32
     return pl.pallas_call(
         kernel,
@@ -411,18 +471,24 @@
             jax.ShapeDtypeStruct((ROWS, 128), f32),
             jax.ShapeDtypeStruct((SHOTS, 128), f32),
         ],
-        in_specs=[hbm, vmem, pl.BlockSpec(memory_space=pltpu.SMEM)],
+        in_specs=[hbm, hbm, pl.BlockSpec(memory_space=pltpu.SMEM)],
         out_specs=[hbm, vmem],
         scratch_shapes=[
             pltpu.VMEM((ROWS, 128), f32),
+            pltpu.VMEM((ROWS, 128), f32),
             pltpu.VMEM((6, 16, SHOTS, 128), f32),
             pltpu.VMEM((ROWS, 128), f32),
-            pltpu.VMEM((2, SHOTS, 128), f32),
-            pltpu.VMEM((2, SHOTS, 128), f32),
+            pltpu.VMEM((16, 128), f32),
+            pltpu.VMEM((2, 16, 128), f32),
+            pltpu.VMEM((16, 128), f32),
+            pltpu.VMEM((8, 16, 128), f32),
+            pltpu.VMEM((16, 128), f32),
+            pltpu.VMEM((SHOTS, 128), f32),
             pltpu.VMEM((8, SHOTS, 128), f32),
             pltpu.VMEM((8, SHOTS, 128), f32),
             pltpu.VMEM((6, SHOTS, 128), f32),
             pltpu.VMEM((6, SHOTS, 128), f32),
+            pltpu.VMEM((PLANES, SHOTS), jnp.int32),
             pltpu.VMEM((SLOPE_ROWS, 8, 128), f32),
             pltpu.VMEM((PLANES + 1, SHOTS, 128), f32),
             pltpu.VMEM((SLOPE_ROWS, 8, 128), f32),
@@ -432,8 +498,10 @@
             pltpu.VMEM((16, 128), jnp.int32),
             pltpu.VMEM((1, 128), f32),
             pltpu.VMEM((32, 128), f32),
-            pltpu.SemaphoreType.DMA((3,)),
-            pltpu.SemaphoreType.DMA((2, 2, GROUPS)),
+            pltpu.SemaphoreType.DMA((2,)),
+            pltpu.SemaphoreType.DMA((1,)),
+            pltpu.SemaphoreType.DMA((GROUPS,)),
+            pltpu.SemaphoreType.DMA((2, 4)),
             pltpu.SemaphoreType.DMA((2, 2, GROUPS)),
             pltpu.SemaphoreType.DMA((2, 3)),
         ],

time: 101 us -> 96.1 us (0.951)
  Pallas kernels: 97.5 us -> 93.9 us
  local copies, waits for them, and re-layouts: 1.25 us -> 0 us
    pallas_call x1, Pallas kernels: 97.5 us -> 93.9 us  [transform(): pl.pallas_call(kernel, out_shape=[jax.ShapeDtypeStruct((ROWS, 128), f32),...]
    unnamed x4 -> x0, local copies, waits for them, and re-layouts: 1.25 us -> none
where the time goes in v3:
time: 96.1 us; the launch traced here: 96 us
  Pallas kernels  93.9 us (98%)
  other arithmetic  1.4 us (1%)
    pallas_call x1, Pallas kernels, transform(): pl.pallas_call(kernel, out_shape=[jax.ShapeDtypeStruct((ROWS, 128), f32),...  93.9 us

profile of v3, /device:TPU:1, one launch (start us, length us, event | category | flops | bytes accessed | tf_op | source)
XLA Modules:
  0.0 96.0 jit_solution(13085616498734651341)
XLA Ops:
  0.7 93.9 %transform.1 = (f32[2048,128]{1,0:T(8,128)S(1)}, f32[32,128]{1,0:T(8,128)S(1)}) custom-call(f32[2048,128]{1,0:T(8,128)} %bitcast.4, s32[8,32]{1,0:T(8,128)} %bitcast.5, s32[1]{0:T(128)S(6)} %copy.4.target_ref), custom_call_target="tpu_custom_call" | custom-call | tf_op jit(solution)/shard_map/transform/pallas_call | solution.py:468
  94.6 1.4 %minimum_subtract_fusion = f32[32,16,4,128]{3,2,1,0:T(4,128)} fusion(f32[32,16,4,128]{3,2,1,0:T(4,128)S(1)} %bitcast.3, f32[32,128]{1,0:T(8,128)S(1)} %neg.4, f32[32,128]{1,0:T(8,128)S(1)} %get-tuple-element.8), kind=kLoop, calls=%fused_computation | loop fusion | flops 786432 | bytes 2129920 | tf_op jit(solution)/shard_map/sub | solution.py:521
  (1 shorter events, 0.0 us)

commit v4 on v3

--- a/solution.py
+++ b/solution.py
@@ -12,7 +12,8 @@
 SHOTS = 32
 GROUPS = 4
 ROWS = 2048
-FIRST = 17
+FIRST = 32
+SECOND = 112
 SLOPE_ROWS = 2**BISECT // 128
 MESH = pl.DeviceIdType.MESH
 
@@ -176,7 +177,8 @@
     def scatter(first, last):
         @pl.loop(first, last)
         def _(i):
-            to = lax.rem(line + i, LINES)
+            near = (i + 1) // 2
+            to = lax.rem(line + jnp.where(i % 2 == 0, 64 - near, 64 + near), LINES)
             remote(
                 x_ref.at[pl.ds(pl.multiple_of(to * 16, 16), 16)],
                 mine,
@@ -186,7 +188,7 @@
                 tm,
             ).start()
 
-    scatter(1, FIRST)
+    scatter(0, FIRST)
 
     band_up.wait_recv()
     band_down.wait_recv()
@@ -204,7 +206,21 @@
         ).start()
     rim_ring[pl.ds(z, 1), :] = rim_merged[pl.ds(z, 1), :]
 
-    scatter(FIRST, LINES)
+    scatter(FIRST, SECOND)
+
+    settle(rim_ring.at[pl.ds(0, 15)], rim_sems.at[1, 3])
+    for k in range(1, 8):
+        remote(
+            rim_ring,
+            rim_plane.at[spot],
+            rim_sems.at[0, 2],
+            rim_sems.at[1, 2],
+            z * 8 + lax.rem(spot + k, 8),
+            tm,
+        ).start()
+    rim_plane[spot] = rim_ring[...]
+
+    scatter(SECOND, LINES - 1)
 
     fetch_rates.wait()
     for row in range(SLOPE_ROWS):
@@ -225,17 +241,6 @@
             total = total + column
         rate_cols[PLANES, group * 8 : group * 8 + 8] = total
 
-    settle(rim_ring.at[pl.ds(0, 15)], rim_sems.at[1, 3])
-    for k in range(1, 8):
-        remote(
-            rim_ring,
-            rim_plane.at[spot],
-            rim_sems.at[0, 2],
-            rim_sems.at[1, 2],
-            z * 8 + lax.rem(spot + k, 8),
-            tm,
-        ).start()
-    rim_plane[spot] = rim_ring[...]
     settle(rim_plane.at[pl.ds(0, 7)], rim_sems.at[1, 2])
     packed = jnp.zeros((16, 128), jnp.float32)
     for k in range(8):
@@ -272,7 +277,7 @@
         )
 
     def group_at(turn):
-        return lax.rem(z // 4 + 3 - turn + GROUPS, GROUPS)
+        return lax.rem(z // 4 + jnp.where(turn == 0, 2, jnp.where(turn == 1, 1, jnp.where(turn == 2, 3, 0))), GROUPS)
 
     @pl.loop(0, GROUPS)
     def _(turn):

time: 96.1 us -> 92.7 us (0.965)
  Pallas kernels: 93.9 us -> 90.5 us
    pallas_call x1, Pallas kernels: 93.9 us -> 90.5 us  [transform(): pl.pallas_call(kernel, out_shape=[jax.ShapeDtypeStruct((ROWS, 128), f32),...]
where the time goes in v4:
time: 92.7 us; the launch traced here: 92.6 us
  Pallas kernels  90.5 us (98%)
  other arithmetic  1.4 us (2%)
    pallas_call x1, Pallas kernels, transform(): pl.pallas_call(kernel, out_shape=[jax.ShapeDtypeStruct((ROWS, 128), f32),...  90.5 us

profile of v4, /device:TPU:1, one launch (start us, length us, event | category | flops | bytes accessed | tf_op | source)
XLA Modules:
  0.0 92.6 jit_solution(11932272554654148142)
XLA Ops:
  0.7 90.5 %transform.1 = (f32[2048,128]{1,0:T(8,128)S(1)}, f32[32,128]{1,0:T(8,128)S(1)}) custom-call(f32[2048,128]{1,0:T(8,128)} %bitcast.4, s32[8,32]{1,0:T(8,128)} %bitcast.5, s32[1]{0:T(128)S(6)} %copy.4.target_ref), custom_call_target="tpu_custom_call" | custom-call | tf_op jit(solution)/shard_map/transform/pallas_call | solution.py:473
  91.2 1.4 %minimum_subtract_fusion = f32[32,16,4,128]{3,2,1,0:T(4,128)} fusion(f32[32,16,4,128]{3,2,1,0:T(4,128)S(1)} %bitcast.3, f32[32,128]{1,0:T(8,128)S(1)} %neg.4, f32[32,128]{1,0:T(8,128)S(1)} %get-tuple-element.8), kind=kLoop, calls=%fused_computation | loop fusion | flops 786432 | bytes 2129920 | tf_op jit(solution)/shard_map/sub | solution.py:526
  (1 shorter events, 0.0 us)

commit v5 on v4

--- a/solution.py
+++ b/solution.py
@@ -41,6 +41,10 @@
 
 def settle(ref, sem):
     pltpu.make_async_copy(ref, ref, sem).wait()
+
+
+def wrap(value, count):
+    return jnp.where(value >= count, value - count, value)
 
 
 def detail(even_part, odd_part, ahead_even):
@@ -72,7 +76,9 @@
     back_send,
     back_recv,
     rate_table,
-    slopes,
+    bars,
+    edges,
+    gain_acc,
     rate_cols,
     kept_acc,
     kept_rows,
@@ -95,11 +101,13 @@
     core = line % 2
     spot = line % 8
 
+    peer_x = [(z * 4 + wrap(x + k, 4)) * 2 for k in range(4)]
+    peer_core = [core, 1 - core]
+    peer_tm = [wrap(tm + k, 4) for k in range(4)]
+
     def plane_peer(step):
         dx, dc, dy = step
-        peer_x = lax.rem(x + dx, 4)
-        peer_core = lax.rem(core + dc, 2)
-        return z * 8 + peer_x * 2 + peer_core, lax.rem(tm + dy, 4)
+        return peer_x[dx] + peer_core[dc], peer_tm[dy]
 
     def plane_index(line_at, tm_at):
         return (line_at % 8) * 4 + tm_at
@@ -115,21 +123,20 @@
     fetch_rates = pltpu.make_async_copy(rates_ref, rate_table, own_sems.at[1])
     fetch_rates.start()
 
-    up = lax.rem(tm + 1, 4)
-    down = lax.rem(tm + 3, 4)
+    up, down = peer_tm[1], peer_tm[3]
     bar = pltpu.get_barrier_semaphore()
 
     @pl.loop(0, 15)
     def _(i):
         near = 8 - (i + 1) // 2
         step = jnp.where(i % 2 == 0, near, 16 - near)
-        plane = lax.rem(z + step, 16) * 8
+        plane = wrap(z + step, 16) * 8
         for k in range(8):
             pl.semaphore_signal(bar, inc=1, device_id=(plane + k, tm), device_id_type=MESH)
 
     for k in range(1, 8):
         pl.semaphore_signal(
-            bar, inc=1, device_id=(z * 8 + lax.rem(spot + k, 8), tm), device_id_type=MESH
+            bar, inc=1, device_id=(z * 8 + wrap(spot + k, 8), tm), device_id_type=MESH
         )
     for to in (up, down):
         pl.semaphore_signal(bar, inc=1, device_id=(line, to), device_id_type=MESH)
@@ -178,7 +185,7 @@
         @pl.loop(first, last)
         def _(i):
             near = (i + 1) // 2
-            to = lax.rem(line + jnp.where(i % 2 == 0, 64 - near, 64 + near), LINES)
+            to = wrap(line + jnp.where(i % 2 == 0, 64 - near, 64 + near), LINES)
             remote(
                 x_ref.at[pl.ds(pl.multiple_of(to * 16, 16), 16)],
                 mine,
@@ -195,7 +202,7 @@
     lane16 = lax.broadcasted_iota(jnp.int32, (16, 128), 1)
     rim_merged[...] = jnp.where(lane16 % 4 < 2, rim_bands[0], rim_bands[1])
     for step in RING_STEPS:
-        to = lax.rem(z + step, 16)
+        to = wrap(z + step, 16)
         remote(
             row_of(rim_merged, to),
             row_of(rim_ring, z),
@@ -215,7 +222,7 @@
             rim_plane.at[spot],
             rim_sems.at[0, 2],
             rim_sems.at[1, 2],
-            z * 8 + lax.rem(spot + k, 8),
+            z * 8 + wrap(spot + k, 8),
             tm,
         ).start()
     rim_plane[spot] = rim_ring[...]
@@ -223,10 +230,6 @@
     scatter(SECOND, LINES - 1)
 
     fetch_rates.wait()
-    for row in range(SLOPE_ROWS):
-        grid_index = (lane + row * 128).astype(jnp.float32)
-        slopes[row] = jnp.exp2(slope_floor + grid_index * (slope_span / 2**BISECT))
-        kept_acc[row] = jnp.zeros((8, 128), jnp.float32)
     for group in range(GROUPS):
         total = jnp.zeros((8, 128), jnp.float32)
         for plane in range(PLANES):
@@ -241,6 +244,16 @@
             total = total + column
         rate_cols[PLANES, group * 8 : group * 8 + 8] = total
 
+    @pl.loop(0, SLOPE_ROWS)
+    def _(row):
+        kept_acc[row] = jnp.zeros((8, 128), jnp.float32)
+        grid_index = (lane + row * 128).astype(jnp.float32)
+        slope = jnp.exp2(slope_floor + grid_index * (slope_span / 2**BISECT))
+        for plane in range(PLANES):
+            for group in range(GROUPS):
+                column = rate_cols[plane, group * 8 : group * 8 + 8]
+                bars[row, plane, group * 8 : group * 8 + 8] = slope * column
+
     settle(rim_plane.at[pl.ds(0, 7)], rim_sems.at[1, 2])
     packed = jnp.zeros((16, 128), jnp.float32)
     for k in range(8):
@@ -254,8 +267,8 @@
     has_next_band = jnp.where(tm < BANDS - 1, 1.0, 0.0)
     has_prev_line = jnp.where(line > 0, 1.0, 0.0)
     has_next_line = jnp.where(line < LINES - 1, 1.0, 0.0)
-    line_up = lax.rem(line + 1, LINES)
-    line_down = lax.rem(line + LINES - 1, LINES)
+    line_up = wrap(line + 1, LINES)
+    line_down = wrap(line + LINES - 1, LINES)
 
     def line_copy(way, group):
         if way == 0:
@@ -277,7 +290,8 @@
         )
 
     def group_at(turn):
-        return lax.rem(z // 4 + jnp.where(turn == 0, 2, jnp.where(turn == 1, 1, jnp.where(turn == 2, 3, 0))), GROUPS)
+        away = jnp.where(turn < 2, turn, 5 - turn)
+        return wrap(z // 4 + away, GROUPS)
 
     @pl.loop(0, GROUPS)
     def _(turn):
@@ -331,55 +345,84 @@
         line_copy(0, group).start()
         line_copy(1, group).start()
 
+    def put(group, r, q, value, gains):
+        wave[pl.ds(group * 512 + r * 4 + q, 8, stride=64), :] = value
+        square = value * value
+        capped = [jnp.minimum(square, 4.0 ** (4 - p)) for p in range(PLANES + 1)]
+        for p in range(PLANES):
+            gains[p] = gains[p] + (capped[p] - capped[p + 1])
+
+    @pl.loop(0, GROUPS)
+    def _(turn):
+        group = group_at(turn)
+        gains = [jnp.zeros((8, 128), jnp.float32) for _ in range(PLANES)]
+        for slot in range(6):
+            values = [lifted[slot, r, span(group)] for r in range(15)]
+            details = [
+                detail(values[2 * i], values[2 * i + 1], values[2 * i + 2]) for i in range(7)
+            ]
+            if slot < 4:
+                for i in range(7):
+                    put(group, 2 * i + 1, slot, details[i], gains)
+            if slot in (0, 2):
+                continue
+            smooths = [None] + [
+                smooth(values[2 * i], details[i - 1], details[i]) for i in range(1, 7)
+            ]
+            if slot < 4:
+                for i in range(1, 7):
+                    put(group, 2 * i, slot, smooths[i], gains)
+                continue
+            second_one = detail(smooths[2], smooths[3], smooths[4])
+            second_two = detail(smooths[4], smooths[5], smooths[6])
+            q = (slot - 4) * 2
+            put(group, 6, q, second_one, gains)
+            put(group, 8, q, smooth(smooths[4], second_one, second_two), gains)
+            put(group, 10, q, second_two, gains)
+            kept_edges = (smooths[1], smooths[2], second_one, smooths[6], second_two)
+            for n, value in enumerate(kept_edges):
+                edges[slot - 4, n, span(group)] = value
+        for p in range(PLANES):
+            gain_acc[p, span(group)] = gains[p]
+
     @pl.loop(0, GROUPS)
     def _(turn):
         group = group_at(turn)
         line_copy(0, group).wait_recv()
         line_copy(1, group).wait_recv()
-        gains = [jnp.zeros((8, 128), jnp.float32) for _ in range(PLANES)]
-
-        def put(r, q, value):
-            wave[pl.ds(group * 512 + r * 4 + q, 8, stride=64), :] = value
-            square = value * value
-            capped = [jnp.minimum(square, 4.0 ** (4 - p)) for p in range(PLANES + 1)]
-            for p in range(PLANES):
-                gains[p] = gains[p] + (capped[p] - capped[p + 1])
-
-        def lift(slot, back_slot, put_odd):
-            values = [lifted[slot, r, span(group)] for r in range(16)]
-            values.append(ahead_recv[slot, span(group)] * has_next_line)
-            details = [
-                detail(values[2 * i], values[2 * i + 1], values[2 * i + 2]) for i in range(8)
+        gains = [gain_acc[p, span(group)] for p in range(PLANES)]
+        for slot in range(6):
+            first, early, third, before, odd, even, last = [
+                lifted[slot, r, span(group)] for r in (0, 1, 2, 12, 13, 14, 15)
             ]
-            if put_odd is not None:
-                for i in range(8):
-                    put(2 * i + 1, put_odd, details[i])
-            if back_slot is None:
-                return None
-            behind = (back_recv[back_slot, span(group)] - 0.5 * values[0]) * has_prev_line
-            chain = [behind] + details
-            smooths = [smooth(values[2 * i], chain[i], chain[i + 1]) for i in range(8)]
-            return smooths, behind, details[7]
-
-        for q in (0, 2):
-            lift(q, None, q)
-        for q, back_slot in ((1, 0), (3, 1)):
-            smooths, _, _ = lift(q, back_slot, q)
-            for i in range(8):
-                put(2 * i, q, smooths[i])
-        for k, q in ((0, 0), (1, 2)):
-            smooths, behind, last = lift(4 + k, 2 + k, None)
-            smooths.append((ahead_recv[6 + k, span(group)] + 0.25 * last) * has_next_line)
-            details = [
-                detail(smooths[2 * i], smooths[2 * i + 1], smooths[2 * i + 2]) for i in range(4)
-            ]
+            ahead = ahead_recv[slot, span(group)] * has_next_line
+            detail_last = detail(even, last, ahead)
+            if slot < 4:
+                put(group, 15, slot, detail_last, gains)
+            if slot in (0, 2):
+                continue
+            back_slot = {1: 0, 3: 1, 4: 2, 5: 3}[slot]
+            behind = (back_recv[back_slot, span(group)] - 0.5 * first) * has_prev_line
+            smooth_first = smooth(first, behind, detail(first, early, third))
+            smooth_last = smooth(even, detail(before, odd, even), detail_last)
+            if slot < 4:
+                put(group, 0, slot, smooth_first, gains)
+                put(group, 14, slot, smooth_last, gains)
+                continue
+            k = slot - 4
+            q = k * 2
+            s1, s2, second_one, s6, second_two = [edges[k, n, span(group)] for n in range(5)]
+            s8 = (ahead_recv[6 + k, span(group)] + 0.25 * detail_last) * has_next_line
+            second_last = detail(s6, smooth_last, s8)
+            second_first = detail(smooth_first, s1, s2)
             behind_two = (
-                back_recv[4 + k, span(group)] + 0.25 * behind - 0.5 * smooths[0]
+                back_recv[4 + k, span(group)] + 0.25 * behind - 0.5 * smooth_first
             ) * has_prev_line
-            chain = [behind_two] + details
-            for i in range(4):
-                put(4 * i, q, smooth(smooths[2 * i], chain[i], chain[i + 1]))
-                put(4 * i + 2, q, details[i])
+            put(group, 0, q, smooth(smooth_first, behind_two, second_first), gains)
+            put(group, 2, q, second_first, gains)
+            put(group, 4, q, smooth(s2, second_first, second_one), gains)
+            put(group, 12, q, smooth(s6, second_two, second_last), gains)
+            put(group, 14, q, second_last, gains)
 
         sums = [
             jnp.broadcast_to(jnp.sum(gains[p], axis=1, keepdims=True), (8, 128))
@@ -389,10 +432,9 @@
 
         @pl.loop(0, SLOPE_ROWS, unroll=4)
         def _(row):
-            slope = slopes[row]
             total = kept_acc[row]
             for p in range(PLANES):
-                total = total + jnp.where(sums[p] >= slope * rates[p], rates[p], 0.0)
+                total = total + jnp.where(sums[p] >= bars[row, p, span(group)], rates[p], 0.0)
             kept_acc[row] = total
 
     out = pltpu.make_async_copy(wave, w_ref, own_sems.at[0])
@@ -421,7 +463,7 @@
             row_of(ring_slots, z),
             tree_sems.at[0, 1],
             tree_sems.at[1, 1],
-            lax.rem(line + step * 8, LINES),
+            wrap(line + step * 8, LINES),
             tm,
         ).start()
     ring_slots[pl.ds(z, 1)] = ring_row[...]
@@ -494,7 +536,9 @@
             pltpu.VMEM((6, SHOTS, 128), f32),
             pltpu.VMEM((6, SHOTS, 128), f32),
             pltpu.VMEM((PLANES, SHOTS), jnp.int32),
-            pltpu.VMEM((SLOPE_ROWS, 8, 128), f32),
+            pltpu.VMEM((SLOPE_ROWS, PLANES, SHOTS, 128), f32),
+            pltpu.VMEM((2, 5, SHOTS, 128), f32),
+            pltpu.VMEM((PLANES, SHOTS, 128), f32),
             pltpu.VMEM((PLANES + 1, SHOTS, 128), f32),
             pltpu.VMEM((SLOPE_ROWS, 8, 128), f32),
             pltpu.VMEM((SLOPE_ROWS, 128), jnp.int32),

time: 92.7 us -> 91.4 us (0.986)
  Pallas kernels: 90.5 us -> 89.2 us
    pallas_call x1, Pallas kernels: 90.5 us -> 89.2 us  [transform(): pl.pallas_call(kernel, out_shape=[jax.ShapeDtypeStruct((ROWS, 128), f32),...]
where the time goes in v5:
time: 91.4 us; the launch traced here: 91.3 us
  Pallas kernels  89.2 us (98%)
  other arithmetic  1.4 us (2%)
    pallas_call x1, Pallas kernels, transform(): pl.pallas_call(kernel, out_shape=[jax.ShapeDtypeStruct((ROWS, 128), f32),...  89.2 us

profile of v5, /device:TPU:1, one launch (start us, length us, event | category | flops | bytes accessed | tf_op | source)
XLA Modules:
  0.0 91.3 jit_solution(9968472776807011911)
XLA Ops:
  0.7 89.2 %transform.1 = (f32[2048,128]{1,0:T(8,128)S(1)}, f32[32,128]{1,0:T(8,128)S(1)}) custom-call(f32[2048,128]{1,0:T(8,128)} %bitcast.4, s32[8,32]{1,0:T(8,128)} %bitcast.5, s32[1]{0:T(128)S(6)} %copy.4.target_ref), custom_call_target="tpu_custom_call" | custom-call | tf_op jit(solution)/shard_map/transform/pallas_call | solution.py:515
  89.9 1.4 %minimum_subtract_fusion = f32[32,16,4,128]{3,2,1,0:T(4,128)} fusion(f32[32,16,4,128]{3,2,1,0:T(4,128)S(1)} %bitcast.3, f32[32,128]{1,0:T(8,128)S(1)} %neg.4, f32[32,128]{1,0:T(8,128)S(1)} %get-tuple-element.8), kind=kLoop, calls=%fused_computation | loop fusion | flops 786432 | bytes 2129920 | tf_op jit(solution)/shard_map/sub | solution.py:570
  (1 shorter events, 0.0 us)

commit v6 on v5

--- a/solution.py
+++ b/solution.py
@@ -22,8 +22,8 @@
 rate_scale = 65536.0
 
 PLANE_STEPS = sorted(
-    [(dx, dc, dy) for dx in range(4) for dc in range(2) for dy in range(4)][1:],
-    key=lambda s: (-(min(s[0], 4 - s[0]) + min(s[2], 4 - s[2])), s),
+    [(dx, dy) for dx in range(4) for dy in range(4)][1:],
+    key=lambda s: (-(min(s[0], 4 - s[0]) + min(s[1], 4 - s[1])), s),
 )
 RING_STEPS = sorted(range(1, 16), key=lambda s: -min(s, 16 - s))
 
@@ -101,16 +101,13 @@
     core = line % 2
     spot = line % 8
 
+    peer_place = [wrap(x + k, 4) * 4 for k in range(4)]
     peer_x = [(z * 4 + wrap(x + k, 4)) * 2 for k in range(4)]
-    peer_core = [core, 1 - core]
     peer_tm = [wrap(tm + k, 4) for k in range(4)]
 
     def plane_peer(step):
-        dx, dc, dy = step
-        return peer_x[dx] + peer_core[dc], peer_tm[dy]
-
-    def plane_index(line_at, tm_at):
-        return (line_at % 8) * 4 + tm_at
+        dx, dy = step
+        return peer_x[dx] + core, peer_tm[dy], peer_place[dx] + peer_tm[dy]
 
     def span(group):
         return pl.ds(pl.multiple_of(group * 8, 8), 8)
@@ -118,7 +115,7 @@
     def row_of(ref, index):
         return ref.at[pl.ds(index, 1)]
 
-    fetch = pltpu.make_async_copy(x_ref, local, own_sems.at[0])
+    fetch = pltpu.make_async_copy(x_ref, local.at[pl.ds(0, ROWS)], own_sems.at[0])
     fetch.start()
     fetch_rates = pltpu.make_async_copy(rates_ref, rate_table, own_sems.at[1])
     fetch_rates.start()
@@ -293,57 +290,60 @@
         away = jnp.where(turn < 2, turn, 5 - turn)
         return wrap(z // 4 + away, GROUPS)
 
+    def lift_time(group, rim, r):
+        at = 4 * r
+        p0, p1, p2, p3 = [
+            held[pl.ds(group * 512 + r * 4 + q, 8, stride=64), :] for q in range(4)
+        ]
+        d1 = detail(p0, p1, p2)
+        ahead = jnp.where(
+            lane == 127,
+            pltpu.roll(rim, 125 - at, 1) * has_next_band,
+            pltpu.roll(p0, 127, 1),
+        )
+        d3 = detail(p2, p3, ahead)
+        rim_detail = pltpu.roll(rim, 128 - at, 1) if at else rim
+        d3_prev = (rim_detail - 0.5 * p0) * has_prev_band
+        s0 = smooth(p0, jnp.where(lane == 0, d3_prev, pltpu.roll(d3, 1, 1)), d1)
+        s2 = smooth(p2, d1, d3)
+        next_s0 = (pltpu.roll(rim, 124 - at, 1) + 0.25 * d3) * has_next_band
+        second = detail(s0, s2, jnp.where(lane == 127, next_s0, pltpu.roll(s0, 127, 1)))
+        rim_second = pltpu.roll(rim, 127 - at, 1)
+        second_prev = (rim_second + 0.25 * d3_prev - 0.5 * s0) * has_prev_band
+        first = smooth(
+            s0, jnp.where(lane == 0, second_prev, pltpu.roll(second, 1, 1)), second
+        )
+        values = (s0, d1, s2, d3, first, second)
+        for slot, value in enumerate(values):
+            lifted[slot, r, span(group)] = value
+        return values
+
     @pl.loop(0, GROUPS)
     def _(turn):
         group = group_at(turn)
         settle(held.at[pl.ds(0, ROWS // GROUPS)], arrive_sems.at[group])
         rim = rims[span(group)]
-        low = []
-        high = []
-        one = []
-        three = []
-        for r in range(16):
-            at = 4 * r
-            p0, p1, p2, p3 = [
-                held[pl.ds(group * 512 + r * 4 + q, 8, stride=64), :] for q in range(4)
-            ]
-            d1 = detail(p0, p1, p2)
-            ahead = jnp.where(
-                lane == 127,
-                pltpu.roll(rim, 125 - at, 1) * has_next_band,
-                pltpu.roll(p0, 127, 1),
-            )
-            d3 = detail(p2, p3, ahead)
-            rim_detail = pltpu.roll(rim, 128 - at, 1) if at else rim
-            d3_prev = (rim_detail - 0.5 * p0) * has_prev_band
-            s0 = smooth(p0, jnp.where(lane == 0, d3_prev, pltpu.roll(d3, 1, 1)), d1)
-            s2 = smooth(p2, d1, d3)
-            next_s0 = (pltpu.roll(rim, 124 - at, 1) + 0.25 * d3) * has_next_band
-            second = detail(s0, s2, jnp.where(lane == 127, next_s0, pltpu.roll(s0, 127, 1)))
-            rim_second = pltpu.roll(rim, 127 - at, 1)
-            second_prev = (rim_second + 0.25 * d3_prev - 0.5 * s0) * has_prev_band
-            first = smooth(
-                s0, jnp.where(lane == 0, second_prev, pltpu.roll(second, 1, 1)), second
-            )
-            for slot, value in enumerate((s0, d1, s2, d3, first, second)):
-                lifted[slot, r, span(group)] = value
-            if r == 0:
-                for slot, value in enumerate((s0, d1, s2, d3, first, second)):
-                    ahead_send[slot, span(group)] = value
-            one.append(d1)
-            three.append(d3)
-            low.append(first)
-            high.append(second)
-        for slot, value in enumerate((low, high)):
+        ends = {r: lift_time(group, rim, r) for r in (0, 1, 2, 10, 11, 12, 13, 14, 15)}
+        for slot, value in enumerate(ends[0]):
+            ahead_send[slot, span(group)] = value
+        for slot, plane in enumerate((4, 5)):
+            value = {r: values[plane] for r, values in ends.items()}
             ahead_send[6 + slot, span(group)] = value[0] + 0.25 * detail(value[0], value[1], value[2])
             d5 = detail(value[10], value[11], value[12])
             d6 = detail(value[12], value[13], value[14])
             s6 = smooth(value[12], d5, d6)
             back_send[4 + slot, span(group)] = value[14] + 0.25 * d6 - 0.5 * s6
-        for slot, value in enumerate((one, three, low, high)):
-            back_send[slot, span(group)] = value[15] - 0.5 * value[14]
+        for slot, plane in enumerate((1, 3, 4, 5)):
+            back_send[slot, span(group)] = ends[15][plane] - 0.5 * ends[14][plane]
         line_copy(0, group).start()
         line_copy(1, group).start()
+
+    @pl.loop(0, GROUPS)
+    def _(turn):
+        group = group_at(turn)
+        rim = rims[span(group)]
+        for r in range(3, 10):
+            lift_time(group, rim, r)
 
     def put(group, r, q, value, gains):
         wave[pl.ds(group * 512 + r * 4 + q, 8, stride=64), :] = value
@@ -437,16 +437,18 @@
                 total = total + jnp.where(sums[p] >= bars[row, p, span(group)], rates[p], 0.0)
             kept_acc[row] = total
 
-    out = pltpu.make_async_copy(wave, w_ref, own_sems.at[0])
+    out = pltpu.make_async_copy(wave.at[pl.ds(0, ROWS)], w_ref, own_sems.at[0])
     out.start()
 
-    kept_rows[...] = jnp.sum(kept_acc[...], axis=1).astype(jnp.int32)
-    place = plane_index(line, tm)
+    half = SLOPE_ROWS // 2
+    kept_rows[:, 0:128] = jnp.sum(kept_acc[0:half], axis=1).astype(jnp.int32)
+    kept_rows[:, 128:256] = jnp.sum(kept_acc[half:SLOPE_ROWS], axis=1).astype(jnp.int32)
+    place = peer_place[0] + tm
 
     for step in PLANE_STEPS:
-        to_line, to_tm = plane_peer(step)
+        to_line, to_tm, to_place = plane_peer(step)
         remote(
-            row_of(kept_rows, plane_index(to_line, to_tm)),
+            row_of(kept_rows, to_place),
             row_of(plane_slots, place),
             tree_sems.at[0, 0],
             tree_sems.at[1, 0],
@@ -454,28 +456,33 @@
             to_tm,
         ).start()
     plane_slots[pl.ds(place, 1)] = kept_rows[pl.ds(place, 1)]
-    settle(plane_slots.at[pl.ds(0, 31)], tree_sems.at[1, 0])
+    settle(held.at[pl.ds(0, 30)], tree_sems.at[1, 0])
     ring_row[...] = jnp.sum(plane_slots[...], axis=0, keepdims=True)
 
-    for step in RING_STEPS:
-        remote(
-            ring_row,
-            row_of(ring_slots, z),
-            tree_sems.at[0, 1],
-            tree_sems.at[1, 1],
-            wrap(line + step * 8, LINES),
-            tm,
-        ).start()
-    ring_slots[pl.ds(z, 1)] = ring_row[...]
-    settle(ring_slots.at[pl.ds(0, 15)], tree_sems.at[1, 1])
+    for step in RING_STEPS + [0]:
+        plane = wrap(z + step, 16) * 8 + spot
+        for to in (plane, plane + 1 - 2 * core):
+            if step == 0 and to is plane:
+                continue
+            remote(
+                ring_row,
+                row_of(ring_slots, z * 2 + core),
+                tree_sems.at[0, 1],
+                tree_sems.at[1, 1],
+                to,
+                tm,
+            ).start()
+    ring_slots[pl.ds(z * 2 + core, 1)] = ring_row[...]
+    settle(held.at[pl.ds(0, 62)], tree_sems.at[1, 1])
     kept = jnp.sum(ring_slots[...], axis=0, keepdims=True)
     limit = target_ref[0] * (SHOTS * LINES * BANDS)
-    grid_row = lax.broadcasted_iota(jnp.int32, (1, 128), 1) + place * 128
+    lane256 = lax.broadcasted_iota(jnp.int32, (1, 256), 1)
+    grid_row = place * 128 + jnp.where(lane256 < 128, lane256, lane256 + 2**BISECT // 2 - 128)
     above = jnp.where((kept > limit) & (grid_row > 0), 1.0, 0.0)
     count_row[...] = jnp.broadcast_to(jnp.sum(above, axis=1, keepdims=True), (1, 128))
 
     for step in PLANE_STEPS:
-        to_line, to_tm = plane_peer(step)
+        to_line, to_tm, _ = plane_peer(step)
         remote(
             count_row,
             row_of(count_slots, place),
@@ -485,7 +492,7 @@
             to_tm,
         ).start()
     count_slots[pl.ds(place, 1)] = count_row[...]
-    settle(count_slots.at[pl.ds(0, 31)], tree_sems.at[1, 2])
+    settle(count_slots.at[pl.ds(0, 15)], tree_sems.at[1, 2])
     chosen = 1.0 + jnp.sum(count_slots[...], axis=0, keepdims=True)
     slope_now = jnp.exp2(slope_floor + chosen * (slope_span / 2**BISECT))
     shrink_ref[...] = jnp.sqrt(slope_now * rate_cols[PLANES] / rate_scale)
@@ -502,9 +509,9 @@
         for way in range(2):
             line_copy(way, group).wait_send()
 
-    settle(plane_slots.at[pl.ds(0, 31)], tree_sems.at[0, 0])
-    settle(ring_slots.at[pl.ds(0, 15)], tree_sems.at[0, 1])
-    settle(count_slots.at[pl.ds(0, 31)], tree_sems.at[0, 2])
+    settle(held.at[pl.ds(0, 30)], tree_sems.at[0, 0])
+    settle(held.at[pl.ds(0, 62)], tree_sems.at[0, 1])
+    settle(count_slots.at[pl.ds(0, 15)], tree_sems.at[0, 2])
 
 
 def transform(rows, rates, byte_target):
@@ -521,16 +528,16 @@
         in_specs=[hbm, hbm, pl.BlockSpec(memory_space=pltpu.SMEM)],
         out_specs=[hbm, vmem],
         scratch_shapes=[
-            pltpu.VMEM((ROWS, 128), f32),
-            pltpu.VMEM((ROWS, 128), f32),
+            pltpu.VMEM((ROWS + 64, 128), f32),
+            pltpu.VMEM((ROWS + 64, 128), f32),
             pltpu.VMEM((6, 16, SHOTS, 128), f32),
-            pltpu.VMEM((ROWS, 128), f32),
+            pltpu.VMEM((ROWS + 64, 128), f32),
             pltpu.VMEM((16, 128), f32),
             pltpu.VMEM((2, 16, 128), f32),
             pltpu.VMEM((16, 128), f32),
             pltpu.VMEM((8, 16, 128), f32),
             pltpu.VMEM((16, 128), f32),
-            pltpu.VMEM((SHOTS, 128), f32),
+            pltpu.VMEM((SHOTS + 8, 128), f32),
             pltpu.VMEM((8, SHOTS, 128), f32),
             pltpu.VMEM((8, SHOTS, 128), f32),
             pltpu.VMEM((6, SHOTS, 128), f32),
@@ -541,12 +548,12 @@
             pltpu.VMEM((PLANES, SHOTS, 128), f32),
             pltpu.VMEM((PLANES + 1, SHOTS, 128), f32),
             pltpu.VMEM((SLOPE_ROWS, 8, 128), f32),
-            pltpu.VMEM((SLOPE_ROWS, 128), jnp.int32),
-            pltpu.VMEM((SLOPE_ROWS, 128), jnp.int32),
-            pltpu.VMEM((1, 128), jnp.int32),
-            pltpu.VMEM((16, 128), jnp.int32),
+            pltpu.VMEM((16, 256), jnp.int32),
+            pltpu.VMEM((16, 256), jnp.int32),
+            pltpu.VMEM((1, 256), jnp.int32),
+            pltpu.VMEM((32, 256), jnp.int32),
             pltpu.VMEM((1, 128), f32),
-            pltpu.VMEM((32, 128), f32),
+            pltpu.VMEM((16, 128), f32),
             pltpu.SemaphoreType.DMA((2,)),
             pltpu.SemaphoreType.DMA((1,)),
             pltpu.SemaphoreType.DMA((GROUPS,)),

time: 91.4 us -> 90.8 us (level)
  no operation moved by 1% of the time
where the time goes in v6:
time: 90.8 us; the launch traced here: 90.7 us
  Pallas kernels  88.6 us (98%)
  other arithmetic  1.4 us (2%)
    pallas_call x1, Pallas kernels, transform(): pl.pallas_call(kernel, out_shape=[jax.ShapeDtypeStruct((ROWS, 128), f32),...  88.6 us

profile of v6, /device:TPU:1, one launch (start us, length us, event | category | flops | bytes accessed | tf_op | source)
XLA Modules:
  0.0 90.7 jit_solution(11016956958742281215)
XLA Ops:
  0.7 88.6 %transform.1 = (f32[2048,128]{1,0:T(8,128)S(1)}, f32[32,128]{1,0:T(8,128)S(1)}) custom-call(f32[2048,128]{1,0:T(8,128)} %bitcast.4, s32[8,32]{1,0:T(8,128)} %bitcast.5, s32[1]{0:T(128)S(6)} %copy.4.target_ref), custom_call_target="tpu_custom_call" | custom-call | tf_op jit(solution)/shard_map/transform/pallas_call | solution.py:522
  89.3 1.4 %minimum_subtract_fusion = f32[32,16,4,128]{3,2,1,0:T(4,128)} fusion(f32[32,16,4,128]{3,2,1,0:T(4,128)S(1)} %bitcast.3, f32[32,128]{1,0:T(8,128)S(1)} %neg.4, f32[32,128]{1,0:T(8,128)S(1)} %get-tuple-element.8), kind=kLoop, calls=%fused_computation | loop fusion | flops 786432 | bytes 2129920 | tf_op jit(solution)/shard_map/sub | solution.py:577
  (1 shorter events, 0.0 us)

commit v7 on v6

--- a/solution.py
+++ b/solution.py
@@ -12,6 +12,7 @@
 SHOTS = 32
 GROUPS = 4
 ROWS = 2048
+CHUNKS = 8
 FIRST = 32
 SECOND = 112
 SLOPE_ROWS = 2**BISECT // 128
@@ -568,13 +569,43 @@
     )(rows, rates, byte_target)
 
 
+def threshold_kernel(wave_ref, shrink_ref, o_ref, out, sems):
+    copies = []
+    for chunk in range(CHUNKS):
+        for shot in range(chunk * SHOTS // CHUNKS, (chunk + 1) * SHOTS // CHUNKS):
+            wavelet = wave_ref[shot * 64 : shot * 64 + 64, :]
+            limit = jnp.broadcast_to(shrink_ref[shot : shot + 1, :], (64, 128))
+            clipped = jnp.minimum(jnp.maximum(wavelet, -limit), limit)
+            out[shot * 64 : shot * 64 + 64, :] = wavelet - clipped
+        rows = pl.ds(chunk * ROWS // CHUNKS, ROWS // CHUNKS)
+        copy = pltpu.make_async_copy(out.at[rows], o_ref.at[rows], sems.at[chunk])
+        copy.start()
+        copies.append(copy)
+    for copy in copies:
+        copy.wait()
+
+
+def threshold(wave, shrink):
+    vmem = pl.BlockSpec(memory_space=pltpu.VMEM)
+    return pl.pallas_call(
+        threshold_kernel,
+        out_shape=jax.ShapeDtypeStruct((ROWS, 128), jnp.float32),
+        in_specs=[vmem, vmem],
+        out_specs=pl.BlockSpec(memory_space=pl.ANY),
+        scratch_shapes=[
+            pltpu.VMEM((ROWS, 128), jnp.float32),
+            pltpu.SemaphoreType.DMA((CHUNKS,)),
+        ],
+        compiler_params=pltpu.CompilerParams(vmem_limit_bytes=24 * 2**20),
+        name="threshold",
+    )(wave, shrink)
+
+
 def body(traces, rates, byte_target):
     width = traces.shape[3]
     rows = traces.reshape(ROWS, width)
     wave, shrink = transform(rows, rates.reshape(PLANES, SHOTS), byte_target)
-    wavelet = wave.reshape(SHOTS, 16, 4, width)
-    shrink_by = shrink[:, None, None, :]
-    return wavelet - jnp.clip(wavelet, -shrink_by, shrink_by)
+    return threshold(wave, shrink).reshape(SHOTS, 16, 4, width)
 
 
 def solution(mesh):

time: 90.8 us -> 90.5 us (level)
  other arithmetic: 1.4 us -> 0 us
  Pallas kernels: 88.6 us -> 89.7 us
    sub x1 -> x0, other arithmetic: 1.4 us -> none  [body(): return wavelet - jnp.clip(wavelet, -shrink_by, shrink_by)]
    pallas_call x0 -> x1, Pallas kernels: none -> 1.05 us  [threshold(): pl.pallas_call(threshold_kernel, out_shape=jax.ShapeDtypeStruct((ROWS, 12...]
where the time goes in v7:
time: 90.5 us; the launch traced here: 90.3 us
  Pallas kernels  89.7 us (99%)
    pallas_call x1, Pallas kernels, transform(): pl.pallas_call(kernel, out_shape=[jax.ShapeDtypeStruct((ROWS, 128), f32),...  88.6 us

profile of v7, /device:TPU:1, one launch (start us, length us, event | category | flops | bytes accessed | tf_op | source)
XLA Modules:
  0.0 90.3 jit_solution(9105052716846535713)
XLA Ops:
  0.7 88.6 %transform.1 = (f32[2048,128]{1,0:T(8,128)S(1)}, f32[32,128]{1,0:T(8,128)S(1)}) custom-call(f32[2048,128]{1,0:T(8,128)} %bitcast.3, s32[8,32]{1,0:T(8,128)} %bitcast.4, s32[1]{0:T(128)S(6)} %copy.4.target_ref), custom_call_target="tpu_custom_call" | custom-call | tf_op jit(solution)/shard_map/transform/pallas_call | solution.py:523
  89.3 1.0 %threshold.1 = f32[2048,128]{1,0:T(8,128)} custom-call(f32[2048,128]{1,0:T(8,128)S(1)} %get-tuple-element.7.wave_ref, f32[32,128]{1,0:T(8,128)S(1)} %get-tuple-element.8.shrink_ref), custom_call_target="tpu_custom_call" | custom-call | tf_op jit(solution)/shard_map/threshold/pallas_call | solution.py:590

commit v8 on v7

--- a/solution.py
+++ b/solution.py
@@ -139,6 +139,29 @@
     for to in (up, down):
         pl.semaphore_signal(bar, inc=1, device_id=(line, to), device_id_type=MESH)
 
+    pl.semaphore_wait(bar, LINES + 1)
+
+    mine = held.at[pl.ds(pl.multiple_of(line * 16, 16), 16)]
+    pltpu.make_async_copy(
+        x_ref.at[pl.ds(pl.multiple_of(line * 16, 16), 16)], mine, arrive_sems.at[z // 4]
+    ).start()
+
+    def scatter(first, last):
+        @pl.loop(first, last)
+        def _(i):
+            near = (i + 1) // 2
+            to = wrap(line + jnp.where(i % 2 == 0, 64 - near, 64 + near), LINES)
+            remote(
+                x_ref.at[pl.ds(pl.multiple_of(to * 16, 16), 16)],
+                mine,
+                send_sem.at[0],
+                arrive_sems.at[z // 4],
+                to,
+                tm,
+            ).start()
+
+    scatter(0, FIRST)
+
     lane = lax.broadcasted_iota(jnp.int32, (8, 128), 1)
     sub = lax.broadcasted_iota(jnp.int32, (8, 128), 0)
     fetch.wait()
@@ -167,33 +190,10 @@
                 total = jnp.where(lane == at, jnp.broadcast_to(column, (8, 128)), total)
         rim_own[pl.ds(plane, 1), :] = jnp.sum(total, axis=0, keepdims=True)
 
-    pl.semaphore_wait(bar, LINES + 1)
-
     band_up = remote(rim_own, rim_bands.at[0], rim_sems.at[0, 0], rim_sems.at[1, 0], line, up)
     band_down = remote(rim_own, rim_bands.at[1], rim_sems.at[0, 1], rim_sems.at[1, 1], line, down)
     band_up.start()
     band_down.start()
-
-    mine = held.at[pl.ds(pl.multiple_of(line * 16, 16), 16)]
-    pltpu.make_async_copy(
-        x_ref.at[pl.ds(pl.multiple_of(line * 16, 16), 16)], mine, arrive_sems.at[z // 4]
-    ).start()
-
-    def scatter(first, last):
-        @pl.loop(first, last)
-        def _(i):
-            near = (i + 1) // 2
-            to = wrap(line + jnp.where(i % 2 == 0, 64 - near, 64 + near), LINES)
-            remote(
-                x_ref.at[pl.ds(pl.multiple_of(to * 16, 16), 16)],
-                mine,
-                send_sem.at[0],
-                arrive_sems.at[z // 4],
-                to,
-                tm,
-            ).start()
-
-    scatter(0, FIRST)
 
     band_up.wait_recv()
     band_down.wait_recv()

time: 90.5 us -> 90.4 us (level)
  no operation moved by 1% of the time
where the time goes in v8:
time: 90.4 us; the launch traced here: 90.3 us
  Pallas kernels  89.7 us (99%)
    pallas_call x1, Pallas kernels, transform(): pl.pallas_call(kernel, out_shape=[jax.ShapeDtypeStruct((ROWS, 128), f32),...  88.6 us

profile of v8, /device:TPU:1, one launch (start us, length us, event | category | flops | bytes accessed | tf_op | source)
XLA Modules:
  0.0 90.3 jit_solution(1125043303536899153)
XLA Ops:
  0.7 88.6 %transform.1 = (f32[2048,128]{1,0:T(8,128)S(1)}, f32[32,128]{1,0:T(8,128)S(1)}) custom-call(f32[2048,128]{1,0:T(8,128)} %bitcast.3, s32[8,32]{1,0:T(8,128)} %bitcast.4, s32[1]{0:T(128)S(6)} %copy.4.target_ref), custom_call_target="tpu_custom_call" | custom-call | tf_op jit(solution)/shard_map/transform/pallas_call | solution.py:523
  89.3 1.0 %threshold.1 = f32[2048,128]{1,0:T(8,128)} custom-call(f32[2048,128]{1,0:T(8,128)S(1)} %get-tuple-element.7.wave_ref, f32[32,128]{1,0:T(8,128)S(1)} %get-tuple-element.8.shrink_ref), custom_call_target="tpu_custom_call" | custom-call | tf_op jit(solution)/shard_map/threshold/pallas_call | solution.py:590
